TPU v7x, 256 devices: a whole 4x4x8 slice. The times are simulated.
256 devices in a mesh: dp: 16 (over z_lo, y, core), feat: 16 (over x, z_hi).
Axes of the slice: x: 4, y: 4, z: 8 (z_hi: 4, z_lo: 2; z = z_hi * 2 + z_lo), core: 2. Of those that a mesh axis runs over, the one named last changes fastest.
Arguments:
- images: bfloat16 [6144, 3072], P('dp'), may hold values from -6 to 6
- labels: int32 [6144], P('dp'), may hold values from 0 to 9
- frequencies: bfloat16 [3072, 16384], P(None, 'feat'), may hold values from -0.15625 to 0.15625
- privacy_noise: float32 [10, 2, 16384], P(None, None, 'feat'), may hold values from -0.6 to 0.6
- latents: bfloat16 [4096, 256], P('dp'), may hold values from -6 to 6
- gen_labels: int32 [4096], P('dp'), may hold values from 0 to 9
- gen_in: bfloat16 [256, 1024], replicated, may hold values from -0.375 to 0.375
- gen_out: bfloat16 [1024, 3072], replicated, may hold values from -0.25 to 0.25
Outputs:
- match_loss: float32 [], replicated
- grad_in: float32 [256, 1024], P('dp')
- grad_out: float32 [1024, 3072], P('dp')
All inputs are finite; a program needn't handle non-finite values.
Results may differ from a plain program's by a relative error of at most 0.0035.
Values sent between devices are 32-bit elements; how exact they have to be, the bound alone decides.
A program may use at most 128 MiB of HBM per device.

v0:
```python
import jax
import jax.numpy as jnp
from jax import lax
from jax.sharding import PartitionSpec as P


def class_sums(phase, classes_of, classes, scale):
    feats = jnp.concatenate([jnp.cos(phase), jnp.sin(phase)], axis=1)
    onehot = (classes_of[:, None] == jnp.arange(classes)[None, :]).astype(jnp.float32)
    sums = jnp.dot(onehot.T, feats, precision=lax.Precision.HIGHEST) * scale
    return (sums.reshape(classes, 2, phase.shape[1]), onehot)


def generator_grads(image_grad, image_out, hidden, pre_hidden, sigmoid_h, latents, gen_out):
    out_grad = (image_grad * (1.0 - image_out * image_out)).astype(jnp.bfloat16)
    grad_out = jnp.einsum("gh,gd->hd", hidden, out_grad, preferred_element_type=jnp.float32)
    back_hidden = jnp.einsum("gd,hd->gh", out_grad, gen_out, preferred_element_type=jnp.float32)
    hidden_grad = (back_hidden * sigmoid_h * (1.0 + pre_hidden * (1.0 - sigmoid_h))).astype(
        jnp.bfloat16
    )
    grad_in = jnp.einsum("gz,gh->zh", latents, hidden_grad, preferred_element_type=jnp.float32)
    return (grad_in, grad_out)


def per_device(images, labels, frequencies, privacy_noise, latents, gen_labels, gen_in, gen_out):
    classes = privacy_noise.shape[0]
    feat_dev = frequencies.shape[1]
    data_devices = lax.axis_size("dp")
    feat_devices = lax.axis_size("feat")
    total_images = images.shape[0] * data_devices
    total_gen = latents.shape[0] * data_devices
    total_feats = feat_dev * feat_devices
    data_phase = jnp.dot(images, frequencies, preferred_element_type=jnp.float32)
    data_part, unused = class_sums(data_phase, labels, classes, classes / total_images)
    pre_hidden = jnp.dot(latents, gen_in, preferred_element_type=jnp.float32)
    sigmoid_h = jax.nn.sigmoid(pre_hidden)
    hidden = (pre_hidden * sigmoid_h).astype(jnp.bfloat16)
    image_out = jnp.tanh(jnp.dot(hidden, gen_out, preferred_element_type=jnp.float32))
    gen_image = image_out.astype(jnp.bfloat16)
    gen_phase = jnp.dot(gen_image, frequencies, preferred_element_type=jnp.float32)
    gen_part, gen_onehot = class_sums(gen_phase, gen_labels, classes, classes / total_gen)
    shares = lax.psum_scatter(data_part, "dp", scatter_dimension=2, tiled=True)
    share_width = feat_dev // data_devices
    noisy = shares + lax.dynamic_slice_in_dim(
        privacy_noise, lax.axis_index("dp") * share_width, share_width, 2
    )
    released = lax.all_gather(noisy, "dp", axis=2, tiled=True)
    mean_gap = lax.psum(gen_part, "dp") - released
    match_loss = lax.psum(jnp.sum(mean_gap * mean_gap), "feat") / (2.0 * total_feats)
    gap_rows = jnp.dot(
        gen_onehot, mean_gap.reshape(classes, 2 * feat_dev), precision=lax.Precision.HIGHEST
    ) * (16.0 * classes / total_gen)
    phase_grad = (
        jnp.cos(gen_phase) * gap_rows[:, feat_dev:] - jnp.sin(gen_phase) * gap_rows[:, :feat_dev]
    ).astype(jnp.bfloat16)
    partial_image = jnp.einsum(
        "gf,df->gd", phase_grad, frequencies, preferred_element_type=jnp.float32
    )
    image_grad = lax.psum(partial_image, "feat")
    grad_in, grad_out = generator_grads(
        image_grad, image_out, hidden, pre_hidden, sigmoid_h, latents, gen_out
    )
    grad_in, grad_out = (
        lax.psum_scatter(grad_in, "dp", scatter_dimension=0, tiled=True),
        lax.psum_scatter(grad_out, "dp", scatter_dimension=0, tiled=True),
    )
    return (match_loss, grad_in, grad_out)


def solution(mesh):
    return jax.shard_map(
        per_device,
        mesh=mesh,
        in_specs=(
            P("dp", None),
            P("dp"),
            P(None, "feat"),
            P(None, None, "feat"),
            P("dp", None),
            P("dp"),
            P(),
            P(),
        ),
        out_specs=(P(), P("dp", None), P("dp", None)),
        check_vma=False,
    )
```

profile of v0, /device:TPU:1, one launch (start us, length us, event | category | flops | bytes accessed | tf_op | source)
XLA Modules:
  0.0 605.7 jit_solution(4414337173241759052)
XLA Ops:
  7.2 1.6 copy-done
  8.8 12.2 %fusion.29 = (f32[384,1024]{1,0:T(8,128)S(1)}, f32[384,1024]{1,0:T(8,128)S(1)}) fusion(bf16[384,3072]{1,0:T(8,128)(2,1)S(1)} %copy-done, bf16[3072,1024]{1,0:T(8,128)(2,1)} %param.10), kind=kOutput, calls=%fused_computation.40 | convolution fusion | flops 2415919104 | bytes 11796480 | tf_op jit(solution)/shard_map/dot_general | solution.py:33
  21.0 1.2 fusion.4
  22.3 5.8 copy.19
  28.1 6.3 %reshape.20 = f32[1024,20]{1,0:T(8,128)} reshape(f32[1024,10,2]{2,1,0:T(8,128)} %bitcast.20) | data formatting | bytes 163840
  34.5 0.3 fusion.31
  34.8 1.0 copy-done.4
  35.8 5.0 convolution_tanh_fusion
  40.8 5.3 fusion.30
  46.1 1.0 copy-done.2
  47.1 0.8 convolution_multiply_fusion.1
  48.0 0.7 reshape.17
  48.7 2.0 copy.15
  50.7 0.2 all-reduce.5.cloned.1.call-start
  51.0 47.3 %reduce-scatter.10.cloned.1.call-done = f32[64,20]{1,0:T(8,128)} async-done(((f32[1024,20]{1,0:T(8,128)}), f32[64,20]{1,0:T(8,128)}) %reduce-scatter.10.cloned.1.call-update) | async-done | bytes 5136
  98.3 1.8 reshape.21
  100.0 1.2 copy.20
  101.3 0.8 dynamic-slice_add_fusion
  102.1 25.1 %all_gather.3 = f32[10,2,1024]{0,1,2:T(2,128)} all-gather(f32[10,2,64]{0,1,2:T(2,128)S(1)} %copy.16), channel_id=1, replica_groups=mesh['dp'=16,'feat'=16] {'dp'}, dimensions={2}, use_global_device_ids=true | all-gather | bytes 87040 | tf_op jit(solution)/shard_map/all_gather | solution.py:47
  127.3 99.2 %all-reduce.3.cloned.1.call-done = f32[10,2,1024]{0,1,2:T(2,128)} async-done(((f32[10,2,1024]{0,1,2:T(2,128)}), f32[10,2,1024]{0,1,2:T(2,128)}) %all-reduce.3.cloned.1.call-update) | async-done | bytes 81936 | tf_op jit(solution)/shard_map/psum | solution.py:48
  226.5 4.1 multiply_reduce_fusion
  230.6 1.4 copy.17
  232.1 1.0 convolution_multiply_fusion
  233.3 6.5 %fusion.19 = f32[256,3072]{1,0:T(8,128)} fusion(bf16[3072,1024]{1,0:T(8,128)(2,1)} %param.10, f32[256,1024]{1,0:T(8,128)S(1)} %copy-done.3, f32[256,2048]{1,0:T(8,128)S(1)} %convolution_multiply_fusion, f32[256,1024]{1,0:T(8,128)S(1)} %get-tuple-element.16), kind=kOutput, calls=%fused_computation.28 | convolution fusion | flops 1611661312 | bytes 13631488 | tf_op jit(solution)/shard_map/gf,df->gd/dot_general | solution.py:56
  239.8 193.3 %all-reduce.5.cloned.1.call-done = f32[256,3072]{1,0:T(8,128)} async-done(((f32[256,3072]{1,0:T(8,128)}), f32[256,3072]{1,0:T(8,128)}) %all-reduce.5.cloned.1.call-update) | async-done | bytes 3145744 | tf_op jit(solution)/shard_map/psum | solution.py:59
  433.1 4.6 multiply_convert_fusion
  437.7 6.6 %convolution_bitcast_fusion = f32[256,1024]{0,1:T(8,128)} fusion(bf16[256,256]{1,0:T(8,128)(2,1)S(1)} %copy-done.8, bf16[256,3072]{1,0:T(8,128)(2,1)} %multiply_convert_fusion, bf16[1024,3072]{1,0:T(8,128)(2,1)} %param.15, f32[256,1024]{1,0:T(8,128)S(1)} %copy-done.5), kind=kOutput, calls=%fused_computation.16 | convolution fusion | flops 1747189760 | bytes 10092544 | tf_op jit(solution)/shard_map/gz,gh->zh/dot_general | solution.py:21
  444.3 2.5 copy.21
  446.8 7.8 %fusion.28 = f32[1024,3072]{1,0:T(8,128)} fusion(bf16[256,3072]{1,0:T(8,128)(2,1)} %multiply_convert_fusion, f32[256,1024]{1,0:T(8,128)S(1)} %copy-done.5), kind=kOutput, calls=%fused_computation.39 | convolution fusion | flops 1611923456 | bytes 15204352 | tf_op jit(solution)/shard_map/gh,gd->hd/dot_general | solution.py:16
  454.7 37.1 %psum.22 = f32[]{:T(128)} all-reduce(f32[]{:T(128)} %get-tuple-element.12), channel_id=1, replica_groups=mesh['dp'=16,'feat'=16] {'feat'}, use_global_device_ids=true, to_apply=%region_3.0 | all-reduce | flops 1 | bytes 8 | tf_op jit(solution)/shard_map/psum | solution.py:49
  492.5 19.5 %reduce-scatter.12.cloned.1.call-done = f32[16,1024]{1,0:T(8,128)} async-done(((f32[256,1024]{1,0:T(8,128)}), f32[16,1024]{1,0:T(8,128)}) %reduce-scatter.12.cloned.1.call-update) | async-done | bytes 65552
  511.9 86.1 %reduce-scatter.8.cloned.1.call-done = f32[64,3072]{1,0:T(8,128)} async-done(((f32[1024,3072]{1,0:T(8,128)}), f32[64,3072]{1,0:T(8,128)}) %reduce-scatter.8.cloned.1.call-update) | async-done | bytes 786448 | tf_op jit(solution)/shard_map/reduce_scatter | solution.py:65
  (37 shorter events, 0.7 us)
Async XLA Ops:
  7.2 1.7 copy-start
  7.2 13.8 %copy-start.10 = (s32[384]{0:T(512)S(1)}, s32[384]{0:T(512)}, u32[]{:S(2)}) copy-start(s32[384]{0:T(512)} %param.9) | copy-start | bytes 4612
  7.2 91.1 %reduce-scatter.10.cloned.1.call-start = ((), (), s32[]{:S(2)}) async-start(), calls=%async_computation.6 | async-start | bytes 557056
  28.1 6.4 %copy-start.6 = (bf16[256,1024]{1,0:T(8,128)(2,1)S(1)}, bf16[256,1024]{1,0:T(8,128)(2,1)}, u32[]{:S(2)}) copy-start(bf16[256,1024]{1,0:T(8,128)(2,1)} %param.14) | copy-start | bytes 1572868
  28.1 6.4 %copy-start.7 = (bf16[256,256]{1,0:T(8,128)(2,1)S(1)}, bf16[256,256]{1,0:T(8,128)(2,1)}, u32[]{:S(2)}) copy-start(bf16[256,256]{1,0:T(8,128)(2,1)} %param.12) | copy-start | bytes 393220
  34.4 192.0 %all-reduce.3.cloned.1.call-start = ((), (), s32[]{:S(2)}) async-start(), calls=%async_computation.3 | async-start | bytes 2097152 | tf_op jit(solution)/shard_map/psum | solution.py:48
  34.5 6.3 %slice-start = ((s8[6291456]{0:T(1024)(128)(4,1)}), s8[4194304]{0:T(1024)(128)(4,1)S(1)}, s32[]{:S(2)}) async-start(s8[6291456]{0:T(1024)(128)(4,1)} %bitcast.21), calls=%async_computation.8 | async-start | bytes 8388608
  34.8 1.0 copy-start.4
  35.8 5.0 slice-start.1
  40.8 5.3 copy-start.1
  40.8 6.3 %copy-start.9 = (s32[256]{0:T(256)S(1)}, s32[256]{0:T(256)}, u32[]{:S(2)}) copy-start(s32[256]{0:T(256)} %param.13) | copy-start | bytes 3076
  46.1 1.0 copy-start.2
  50.7 382.3 %all-reduce.5.cloned.1.call-start = ((), (), s32[]{:S(2)}) async-start(), calls=%async_computation.4 | async-start | bytes 6291456 | tf_op jit(solution)/shard_map/psum | solution.py:59
  232.0 1.2 copy-start.3
  239.7 197.9 %copy-start.5 = (f32[256,1024]{1,0:T(8,128)S(1)}, f32[256,1024]{1,0:T(8,128)}, u32[]{:S(2)}) copy-start(f32[256,1024]{1,0:T(8,128)} %copy-done.4) | copy-start | bytes 3145732
  239.7 197.9 %copy-start.8 = (bf16[256,256]{1,0:T(8,128)(2,1)S(1)}, bf16[256,256]{1,0:T(8,128)(2,1)}, u32[]{:S(2)}) copy-start(bf16[256,256]{1,0:T(8,128)(2,1)} %param.12) | copy-start | bytes 393220
  239.8 272.2 %reduce-scatter.12.cloned.1.call-start = ((), (), s32[]{:S(2)}) async-start(), calls=%async_computation.7 | async-start | bytes 1114112
  446.8 151.2 %reduce-scatter.8.cloned.1.call-start = ((), (), s32[]{:S(2)}) async-start(), calls=%async_computation.5 | async-start | bytes 13369344 | tf_op jit(solution)/shard_map/reduce_scatter | solution.py:65
Sparse Core Ops, SparseCore 0:
  34.5 63.6 reduce-scatter.9
  101.1 125.3 all-reduce.2
  239.9 193.1 all-reduce.4
  446.9 64.9 reduce-scatter.11
  515.1 82.8 reduce-scatter.7
where the time goes:
time: 609 us; the launch traced here: 606 us
  waiting for transfers between devices  445 us (73%)
  blocking collectives  62.3 us (10%)
  matrix products  46.6 us (8%)
  local copies, waits for them, and re-layouts  25.8 us (4%)
  between operations  15.8 us (3%)
  other arithmetic  9.52 us (2%)
    psum x1, waiting for transfers between devices, per_device(): image_grad = lax.psum(partial_image, 'feat')  193 us
    psum x1, waiting for transfers between devices, per_device(): mean_gap = lax.psum(gen_part, 'dp') - released  99.2 us
    reduce_scatter x1, waiting for transfers between devices, per_device(): lax.psum_scatter(grad_out, 'dp', scatter_dimension=0, tiled=True)  86.1 us
    unnamed x7, waiting for transfers between devices  66.9 us
    psum x1, blocking collectives, per_device(): lax.psum(jnp.sum(mean_gap * mean_gap), 'feat') / (2.0 * total_feats)  37.1 us
    all_gather x1, blocking collectives, per_device(): released = lax.all_gather(noisy, 'dp', axis=2, tiled=True)  25.1 us
    unnamed x33, local copies, waits for them, and re-layouts  21.4 us
  transfers between devices with their start and end apart: 5, of which 5 were waited for; matrix products, arithmetic and copies ran while one was open for 4% of the time, Pallas kernels for 0%

commit v1 on v0

v1 whole, which is shorter than its diff:
```python
import functools

import jax
import jax.numpy as jnp
from jax import lax
from jax.experimental import pallas as pl
from jax.experimental.pallas import tpu as pltpu
from jax.sharding import PartitionSpec as P

MESH = pl.DeviceIdType.MESH
F32 = jnp.float32
BF16 = jnp.bfloat16

SIN = (6.28318284102346, -41.34142273936724, 81.59620932441723, -76.58030929887768, 41.20616782312917, -12.272323133322006)
COS = (0.999999989172567, -19.73920453212146, 64.93911898457917, -85.45016555726593, 60.16783176141255, -25.968313346422505, 6.5296104065360066)

N, D, FL, HID, Z, NI = 256, 3072, 1024, 1024, 256, 384
ROWS = N + NI
SUBS = (96, 96)
STARTS = (0, 96)
NS = len(SUBS)
Q = 4 * NS
LAG = 2
NT = (((1,), (1,)), ((), ()))


def poly(coeffs, u):
    r = coeffs[-1] * u + coeffs[-2]
    for c in coeffs[-3::-1]:
        r = r * u + c
    return r


def cos_sin(phase):
    t = phase * 0.15915494309189535
    f = t - jnp.round(t)
    u = f * f
    return poly(COS, u), f * poly(SIN, u)


def split(v):
    hi = v.astype(BF16)
    return hi, (v - hi.astype(F32)).astype(BF16)


def mm(a, b):
    return jnp.dot(a, b, preferred_element_type=F32)


def mmt(a, b):
    return lax.dot_general(a, b, NT, preferred_element_type=F32)


def kernel(images_h, freq_h, gen_out_h, lab_ref, glab_ref, noise_ref, lat_ref, gin_ref,
           loss_ref, gi_ref, go_ref,
           freq, gout, lhs, noise, hidden, q_s, qt, s_s, st, latt, oneh, onet, cosg, sing, gp, rsb, gapb, pg,
           part, ohi, olo, hgt, gin, xa, xb, za, zb, gic, gid, gix, giz, gig, lvx, lvz, gt_p, goc, god, gfull,
           lsem, ar_s, ar_r, xa_s, xa_r, xb_s, xb_r, za_s, za_r, zb_s, zb_r, g1_s, g1_r, gd_s, gd_r,
           gx_s, gx_r, gz_s, gz_r, gzg_s, gzg_r, gxg_s, gxg_r, lx_s, lx_r, lz_s, lz_r,
           oc_s, oc_r, od_s, od_r, oz_s, oz_r, ox_s, ox_r, oe_s, oe_r):
    dp = lax.axis_index("dp")
    ft = lax.axis_index("feat")
    core = lax.rem(dp, 2)
    chip = dp // 2
    x = ft // 4
    zh = lax.rem(ft, 4)

    def xdev(k):
        return (dp, lax.rem(x + k, 4) * 4 + zh)

    def zdev(k):
        return (dp, x * 4 + lax.rem(zh + k, 4))

    def cdev(k):
        return (lax.rem(chip + k, 8) * 2 + core, ft)

    other = (chip * 2 + 1 - core, ft)

    def remote(src, dst, ss, rs, dev):
        return pltpu.make_async_remote_copy(src_ref=src, dst_ref=dst, send_sem=ss, recv_sem=rs, device_id=dev, device_id_type=MESH)

    loads = [pltpu.make_async_copy(gen_out_h, gout, lsem.at[0]), pltpu.make_async_copy(images_h, lhs.at[pl.ds(N, NI)], lsem.at[1])]
    for n in range(4):
        loads.append(pltpu.make_async_copy(freq_h.at[:, pl.ds(n * 256, 256)], freq.at[:, pl.ds(n * 256, 256)], lsem.at[2 + n]))
    for c in loads:
        c.start()

    bar = pltpu.get_barrier_semaphore()

    def greet_dp(k, carry):
        pl.semaphore_signal(bar, inc=1, device_id=(lax.rem(dp + k, 16), ft), device_id_type=MESH)
        return carry

    lax.fori_loop(1, 16, greet_dp, 0)
    for k in (1, 2, 3):
        pl.semaphore_signal(bar, inc=1, device_id=xdev(k), device_id_type=MESH)
        pl.semaphore_signal(bar, inc=1, device_id=zdev(k), device_id_type=MESH)

    noise[...] = jnp.zeros_like(noise)
    for k in range(2):
        noise[16 * k : 16 * k + 10, :] = noise_ref[:, k, :]
    cls = lax.broadcasted_iota(jnp.int32, (32, N), 0)
    on_g = (jnp.where(cls < 16, cls, cls - 16) == glab_ref[...]).astype(F32)
    cls_g = lax.broadcasted_iota(jnp.int32, (16, N), 0)
    oneh[0:16, 0:N] = (cls_g == glab_ref[...]).astype(F32).astype(BF16)
    oneh[16:32, 0:N] = jnp.zeros((16, N), BF16)
    cls_d = lax.broadcasted_iota(jnp.int32, (16, NI), 0)
    oneh[0:16, N:ROWS] = jnp.zeros((16, NI), BF16)
    oneh[16:32, N:ROWS] = (cls_d == lab_ref[...]).astype(F32).astype(BF16)
    onet[...] = jnp.concatenate([on_g, jnp.zeros((96, N), F32)], axis=0).T.astype(BF16)
    latt[...] = lat_ref[...].astype(F32).T.astype(BF16)

    pre = mm(lat_ref[...], gin_ref[...])
    sig = jax.nn.sigmoid(pre)
    hidden[...] = (pre * sig).astype(BF16)
    s_s[...] = sig * (1.0 + pre * (1.0 - sig))
    loads[0].wait()

    def gen(n, carry):
        cols = pl.ds(pl.multiple_of(n * 512, 512), 512)
        out = jnp.tanh(mm(hidden[...], gout[:, cols]))
        lhs[0:N, cols] = out.astype(BF16)
        q_s[:, cols] = 1.0 - out * out
        return carry

    lax.fori_loop(0, 6, gen, 0)
    loads[1].wait()

    def phases(n):
        loads[2 + n].wait()
        cols = slice(n * 256, n * 256 + 256)
        ph = mm(lhs[...], freq[:, cols])
        cs, sn = cos_sin(ph)
        cosg[:, cols] = cs[0:N]
        sing[:, cols] = sn[0:N]
        for k, v in ((0, cs), (1, sn)):
            hi, lo = split(v)
            sums = mm(oneh[...], hi) + mm(oneh[...], lo)
            gp[16 * k : 16 * k + 16, cols] = sums[0:16] * (10.0 / 4096.0) - sums[16:32] * (10.0 / 6144.0)

    def block(o):
        return pl.multiple_of(8 * (o // 4), 8), pl.multiple_of(128 * lax.rem(o, 4), 128)

    row_me, lane_me = block(dp)

    def rs_copy(h, peer):
        r, l = block(peer)
        src = gp.at[pl.ds(r, 8), pl.ds(pl.multiple_of(h * 512 + l, 128), 128)]
        return src

    def ar_send(h):
        rsb[h, dp] = gp[pl.ds(row_me, 8), pl.ds(pl.multiple_of(h * 512 + lane_me, 128), 128)]

        def go(k, carry):
            peer = lax.rem(dp + k, 16)
            remote(rs_copy(h, peer), rsb.at[h, dp], ar_s.at[h, 0, peer], ar_r.at[h, 0, dp], (peer, ft)).start()
            return carry

        lax.fori_loop(1, 16, go, 0)

    def ar_wait(h, which):
        def go(k, carry):
            peer = lax.rem(dp + k, 16)
            if which == 0:
                d = remote(rs_copy(h, peer), rsb.at[h, peer], ar_s.at[h, 0, peer], ar_r.at[h, 0, peer], (peer, ft))
            else:
                r, l = block(peer)
                d = remote(gapb.at[h, pl.ds(row_me, 8), pl.ds(lane_me, 128)], gapb.at[h, pl.ds(r, 8), pl.ds(l, 128)],
                           ar_s.at[h, 1, peer], ar_r.at[h, 1, peer], (peer, ft))
            d.wait_recv()
            d.wait_send()
            return carry

        lax.fori_loop(1, 16, go, 0)

    def ar_spread(h):
        ar_wait(h, 0)
        mine = gapb.at[h, pl.ds(row_me, 8), pl.ds(lane_me, 128)]
        mine[...] = jnp.sum(rsb[h], axis=0)

        def go(k, carry):
            peer = lax.rem(dp + k, 16)
            remote(mine, mine, ar_s.at[h, 1, peer], ar_r.at[h, 1, dp], (peer, ft)).start()
            return carry

        lax.fori_loop(1, 16, go, 0)

    def gap(h):
        ar_wait(h, 1)
        cols = slice(h * 512, h * 512 + 512)
        g = gapb[h] - noise[:, cols]
        sq = g * g
        lv = sq[0:8] + sq[8:16] + sq[16:24] + sq[24:32]
        lv = lv[:, 0:128] + lv[:, 128:256] + lv[:, 256:384] + lv[:, 384:512]
        hi, lo = split(g * (160.0 / 4096.0))
        g0 = mm(onet[:, 0:32], jnp.concatenate([hi[0:16], lo[0:16]], axis=0))
        g1 = mm(onet[:, 0:32], jnp.concatenate([hi[16:32], lo[16:32]], axis=0))
        pg[:, cols] = (cosg[:, cols] * g1 - sing[:, cols] * g0).astype(BF16)
        return lv

    phases(0)
    phases(1)
    pl.semaphore_wait(bar, 21)
    ar_send(0)
    phases(2)
    ar_spread(0)
    phases(3)
    ar_send(1)

    def turn_q(n, carry):
        o = pl.multiple_of(n * 256, 256)
        qt[pl.ds(o, 256), :] = q_s[:, pl.ds(o, 256)].T
        return carry

    lax.fori_loop(0, 12, turn_q, 0)
    lv = gap(0)

    def first_half(n, carry):
        rows = pl.ds(pl.multiple_of(n * 768, 256), 768)
        part[rows, :] = mmt(freq[rows, 0:512], pg[:, 0:512])
        return carry

    lax.fori_loop(0, 4, first_half, 0)
    ar_spread(1)

    def turn_s(n, carry):
        o = pl.multiple_of(n * 256, 256)
        st[pl.ds(o, 256), :] = s_s[:, pl.ds(o, 256)].T
        return carry

    lax.fori_loop(0, 4, turn_s, 0)
    lv = lv + gap(1)

    def part_rows(xr, k, s, half, rows):
        zq = lax.rem(zh + (2, 1, 3, 0)[k], 4)
        base = lax.rem(x + xr, 4) * 768 + zq * 192 + STARTS[s] + half
        return part.at[pl.ds(pl.multiple_of(base, 8), rows), :]

    def second_half(xr):
        rows = pl.ds(pl.multiple_of(lax.rem(x + xr, 4) * 768, 256), 768)
        part[rows, :] += mmt(freq[rows, 512:1024], pg[:, 512:1024])

    def qk(q):
        return q // 4, q % 4

    def xa_copy(q, b):
        s, k = qk(q)
        w = SUBS[s] // 2
        return remote(part_rows(2, k, s, b * w, w), xa.at[q, b, pl.ds(0, w)], xa_s.at[q, b], xa_r.at[q, b], xdev((1, 3)[b]))

    def xb_copy(q, b):
        s, k = qk(q)
        w = SUBS[s]
        return remote(part_rows((1, 3)[b], k, s, 0, w), xb.at[q, b, pl.ds(0, w)], xb_s.at[q, b], xb_r.at[q, b], xdev((1, 3)[b]))

    def za_copy(s, b):
        w = SUBS[s] // 2
        return remote(part_rows(0, 0, s, b * w, w), za.at[s, b, pl.ds(0, w)], za_s.at[s, b], za_r.at[s, b], zdev((1, 3)[b]))

    def zb_copy(s, b):
        w = SUBS[s]
        return remote(part_rows(0, 1 + b, s, 0, w), zb.at[s, b, pl.ds(0, w)], zb_s.at[s, b], zb_r.at[s, b], zdev((1, 3)[b]))

    sent = []
    second_half(2)
    for q in range(Q):
        for b in range(2):
            c = xa_copy(q, b)
            c.start()
            sent.append(c)

    lvx[x] = lv
    for k in (1, 2, 3):
        peer = lax.rem(x + k, 4)
        c = remote(lvx.at[x], lvx.at[x], lx_s.at[peer], lx_r.at[x], xdev(k))
        c.start()
        sent.append(c)

    for xr in (1, 3, 0):
        second_half(xr)

    def factor(n, carry):
        rows = pl.ds(pl.multiple_of(n * 256, 256), 256)
        hi, lo = split(part[rows, :] * qt[rows, :])
        ohi[rows, :] = hi
        olo[rows, :] = lo
        return carry

    lax.fori_loop(0, 12, factor, 0)

    def s2(q):
        s, k = qk(q)
        w = SUBS[s] // 2
        for b in range(2):
            xa_copy(q, b).wait_recv()
            r = part_rows((1, 3)[b], k, s, b * w, w)
            r[...] = r[...] + xa[q, b, 0:w]
            c = xb_copy(q, b)
            c.start()
            sent.append(c)

    def s3(q):
        s, k = qk(q)
        w = SUBS[s]
        h = w // 2
        for b in range(2):
            xb_copy(q, b).wait_recv()
        r = part_rows(0, k, s, 0, w)
        r[...] = r[...] + xb[q, 0, 0:w] + xb[q, 1, 0:w]
        if k == 0:
            for b in range(2):
                c = za_copy(s, b)
                c.start()
                sent.append(c)
        elif k < 3:
            b = k - 1
            za_copy(s, b).wait_recv()
            r = part_rows(0, k, s, b * h, h)
            r[...] = r[...] + za[s, b, 0:h]
            c = zb_copy(s, b)
            c.start()
            sent.append(c)
        else:
            for b in range(2):
                zb_copy(s, b).wait_recv()
            own = r[...] + zb[s, 0, 0:w] + zb[s, 1, 0:w]
            base = pl.multiple_of(ft * 192 + STARTS[s], 8)
            og = (own * qt[pl.ds(base, w), :]).astype(BF16)
            gt_p[s, 0:w, :] = mm(og, hidden[...])
            c = oc_copy(s)
            c.start()
            sent.append(c)

    def oc_copy(s):
        h = SUBS[s] // 2
        return remote(gt_p.at[s, pl.ds(pl.multiple_of((1 - core) * h, 8), h)], goc.at[s, pl.ds(0, h)], oc_s.at[s], oc_r.at[s], other)

    def od_copy(s, k, mine):
        h = SUBS[s] // 2
        peer = lax.rem(chip + k, 8)
        return remote(gt_p.at[s, pl.ds(pl.multiple_of(core * h, 8), h), pl.ds(pl.multiple_of(peer * 128, 128), 128)],
                      god.at[s, chip if mine else peer, pl.ds(0, h)], od_s.at[s, peer], od_r.at[s, chip if mine else peer], cdev(k))

    def rows_of(s, c):
        h = SUBS[s] // 2
        return pl.ds(pl.multiple_of(STARTS[s] + c * h, 8), h)

    def oz_copy(s, k, mine):
        peer = lax.rem(zh + k, 4)
        src = zh if mine else peer
        at = gfull.at[x * 4 + src, rows_of(s, core), :]
        return remote(at, at, oz_s.at[s, peer], oz_r.at[s, src], zdev(k))

    def ox_copy(s, k, mine):
        peer = lax.rem(x + k, 4)
        src = x if mine else peer
        at = gfull.at[pl.ds(src * 4, 4), rows_of(s, core), :]
        return remote(at, at, ox_s.at[s, peer], ox_r.at[s, src], xdev(k))

    def oe_copy(s, c):
        at = gfull.at[:, rows_of(s, c), :]
        return remote(at, at, oe_s.at[s], oe_r.at[s], other)

    def start_all(copies):
        for c in copies:
            c.start()
            sent.append(c)

    def go1(s):
        h = SUBS[s] // 2
        oc_copy(s).wait_recv()
        r = gt_p.at[s, pl.ds(pl.multiple_of(core * h, 8), h)]
        r[...] = r[...] + goc[s, 0:h]
        start_all([od_copy(s, k, True) for k in range(1, 8)])
        god[s, chip, 0:h] = gt_p[s, pl.ds(pl.multiple_of(core * h, 8), h), pl.ds(pl.multiple_of(chip * 128, 128), 128)]

    def go2(s):
        h = SUBS[s] // 2
        for k in range(1, 8):
            od_copy(s, k, False).wait_recv()
        gfull[ft, rows_of(s, core), :] = jnp.sum(god[s, :, 0:h], axis=0)
        start_all([oz_copy(s, k, True) for k in (1, 3, 2)])

    def go3(s):
        for k in (1, 3, 2):
            oz_copy(s, k, False).wait_recv()
        start_all([ox_copy(s, k, True) for k in (1, 3, 2)])

    def go4(s):
        for k in (1, 3, 2):
            ox_copy(s, k, False).wait_recv()
        start_all([oe_copy(s, core)])

    def back(n, carry):
        rows = pl.ds(pl.multiple_of(n * 256, 256), 256)
        bh = mm(gout[rows, :], ohi[...]) + mm(gout[rows, :], olo[...])
        hi, lo = split(bh * st[rows, :])
        g = mmt(latt[...], hi) + mmt(latt[...], lo)
        gin[:, :, :, rows] = g.reshape(8, 2, 16, 256)
        return carry

    def gi0():
        lax.fori_loop(0, 4, back, 0)
        start_all([g1_copy()])

    def g1_copy():
        return remote(gin.at[:, 1 - core], gic, g1_s.at[0], g1_r.at[0], other)

    def gd_copy(k, mine):
        peer = lax.rem(chip + k, 8)
        src = chip if mine else peer
        return remote(gin.at[peer, core], gid.at[src], gd_s.at[peer], gd_r.at[src], cdev(k))

    def gi1():
        g1_copy().wait_recv()
        gin[:, core] = gin[:, core] + gic[...]
        start_all([gd_copy(k, True) for k in range(1, 8)])
        gid[chip] = gin[chip, core]

    def gx_copy(k, mine):
        peer = lax.rem(x + k, 4)
        src = x if mine else peer
        return remote(gid.at[chip, :, pl.ds(pl.multiple_of(peer * 256, 256), 256)], gix.at[src], gx_s.at[peer], gx_r.at[src], xdev(k))

    def gi2():
        for k in range(1, 8):
            gd_copy(k, False).wait_recv()
        total = jnp.sum(gid[...], axis=0)
        gid[chip] = total
        start_all([gx_copy(k, True) for k in (1, 3, 2)])
        gix[x] = gid[chip, :, pl.ds(pl.multiple_of(x * 256, 256), 256)]
        for k in (1, 2, 3):
            peer = lax.rem(x + k, 4)
            remote(lvx.at[x], lvx.at[peer], lx_s.at[peer], lx_r.at[peer], xdev(k)).wait_recv()
        lvz[zh] = jnp.sum(lvx[...], axis=0)
        for k in (1, 2, 3):
            peer = lax.rem(zh + k, 4)
            start_all([remote(lvz.at[zh], lvz.at[zh], lz_s.at[peer], lz_r.at[zh], zdev(k))])

    def zblock(p):
        return pl.ds(pl.multiple_of(8 * (p // 2), 8), 8), pl.ds(pl.multiple_of(128 * lax.rem(p, 2), 128), 128)

    def gz_copy(k, mine):
        peer = lax.rem(zh + k, 4)
        src = zh if mine else peer
        r, l = zblock(peer)
        return remote(gix.at[x, r, l], giz.at[src], gz_s.at[peer], gz_r.at[src], zdev(k))

    def gi3():
        for k in (1, 3, 2):
            gx_copy(k, False).wait_recv()
        total = jnp.sum(gix[...], axis=0)
        gix[x] = total
        start_all([gz_copy(k, True) for k in (1, 3, 2)])
        r, l = zblock(zh)
        giz[zh] = gix[x, r, l]

    def gzg_copy(k, mine):
        peer = lax.rem(zh + k, 4)
        src = zh if mine else peer
        r, l = zblock(src)
        return remote(gig.at[x, r, l], gig.at[x, r, l], gzg_s.at[peer], gzg_r.at[src], zdev(k))

    def gi4():
        for k in (1, 3, 2):
            gz_copy(k, False).wait_recv()
        r, l = zblock(zh)
        gig[x, r, l] = jnp.sum(giz[...], axis=0)
        start_all([gzg_copy(k, True) for k in (1, 3, 2)])

    def gxg_copy(k, mine):
        peer = lax.rem(x + k, 4)
        src = x if mine else peer
        return remote(gig.at[src], gig.at[src], gxg_s.at[peer], gxg_r.at[src], xdev(k))

    def gi5():
        for k in (1, 3, 2):
            gzg_copy(k, False).wait_recv()
        start_all([gxg_copy(k, True) for k in (1, 3, 2)])

    def gi6():
        for k in (1, 3, 2):
            gxg_copy(k, False).wait_recv()
        for p in range(4):
            gi_ref[:, p * 256 : p * 256 + 256] = gig[p]
        for k in (1, 2, 3):
            peer = lax.rem(zh + k, 4)
            remote(lvz.at[zh], lvz.at[peer], lz_s.at[peer], lz_r.at[peer], zdev(k)).wait_recv()
        loss_ref[...] = jnp.sum(jnp.sum(lvz[...], axis=0), axis=(0, 1), keepdims=True) * (1.0 / 32768.0)

    gi0()
    s2(0)
    s2(1)
    gi1()
    s2(2)
    s3(0)
    s2(3)
    s3(1)
    s2(4)
    s3(2)
    s2(5)
    s3(3)
    s2(6)
    s3(4)
    gi2()
    go1(0)
    s2(7)
    s3(5)
    gi3()
    go2(0)
    s3(6)
    s3(7)
    go1(1)
    gi4()
    go3(0)
    gi5()
    go2(1)
    go4(0)
    gi6()
    go3(1)
    go4(1)
    for s in range(NS):
        oe_copy(s, 1 - core).wait_recv()

    def turn(p, carry):
        v = gfull[pl.ds(p * 2, 2)].reshape(384, 128).T
        go_ref[:, pl.ds(pl.multiple_of(p * 384, 128), 384)] = jnp.where(core == 0, v[0:64], v[64:128])
        return carry

    lax.fori_loop(0, 8, turn, 0)
    for c in sent:
        c.wait_send()


def per_device(images, labels, frequencies, privacy_noise, latents, gen_labels, gen_in, gen_out):
    vm = pl.BlockSpec(memory_space=pltpu.VMEM)
    hb = pl.BlockSpec(memory_space=pltpu.HBM)
    V = pltpu.VMEM
    dma = pltpu.SemaphoreType.DMA
    w = max(SUBS)
    h = w // 2
    scratch = [
        V((D, FL), BF16), V((HID, D), BF16), V((ROWS, D), BF16), V((32, FL), F32), V((N, HID), BF16),
        V((N, D), F32), V((D, N), F32), V((N, HID), F32), V((HID, N), F32), V((Z, N), BF16),
        V((32, ROWS), BF16), V((N, 128), BF16), V((N, FL), F32), V((N, FL), F32), V((32, FL), F32),
        V((2, 16, 8, 128), F32), V((2, 32, 512), F32), V((N, FL), BF16),
        V((D, N), F32), V((D, N), BF16), V((D, N), BF16), V((8, 128), F32), V((8, 2, 16, HID), F32),
        V((Q, 2, h, N), F32), V((Q, 2, w, N), F32), V((NS, 2, h, N), F32), V((NS, 2, w, N), F32),
        V((8, 16, HID), F32), V((8, 16, HID), F32), V((4, 16, 256), F32), V((4, 8, 128), F32), V((4, 16, 256), F32),
        V((4, 8, 128), F32), V((4, 8, 128), F32),
        V((NS, w, HID), F32), V((NS, h, HID), F32), V((NS, 8, h, 128), F32), V((16, 192, 128), F32),
    ]
    two = lambda *s: [dma(s), dma(s)]
    sems = [dma((6,))] + two(2, 2, 16) + two(Q, 2) + two(Q, 2) + two(NS, 2) + two(NS, 2)
    sems += two(1) + two(8) + two(4) + two(4) + two(4) + two(4) + two(4) + two(4)
    sems += two(NS) + two(NS, 8) + two(NS, 4) + two(NS, 4) + two(NS)
    loss, gi, go = pl.pallas_call(
        kernel,
        out_shape=(
            jax.ShapeDtypeStruct((1, 1), F32),
            jax.ShapeDtypeStruct((16, HID), F32),
            jax.ShapeDtypeStruct((64, D), F32),
        ),
        in_specs=[hb, hb, hb, vm, vm, vm, vm, vm],
        out_specs=(vm, vm, vm),
        scratch_shapes=scratch + sems,
        compiler_params=pltpu.CompilerParams(collective_id=0, has_side_effects=True, vmem_limit_bytes=58 << 20),
        cost_estimate=pl.CostEstimate(flops=12_000_000_000, bytes_accessed=17_000_000, transcendentals=2_000_000),
        name="feature_match",
    )(images, frequencies, gen_out, labels.reshape(1, NI), gen_labels.reshape(1, N), privacy_noise, latents, gen_in)
    return loss.reshape(()), gi, go


def solution(mesh):
    return jax.shard_map(
        per_device,
        mesh=mesh,
        in_specs=(
            P("dp", None),
            P("dp"),
            P(None, "feat"),
            P(None, None, "feat"),
            P("dp", None),
            P("dp"),
            P(),
            P(),
        ),
        out_specs=(P(), P("dp", None), P("dp", None)),
        check_vma=False,
    )
```

time: 609 us -> 111 us (0.18)
  waiting for transfers between devices: 445 us -> 0 us
  Pallas kernels: 0 us -> 104 us
  blocking collectives: 62.3 us -> 0 us
  matrix products: 46.6 us -> 0 us
  local copies, waits for them, and re-layouts: 25.8 us -> 4.79 us
  between operations: 15.8 us -> 2.39 us
  other arithmetic: 9.52 us -> 0 us
    psum x2 -> x0, waiting for transfers between devices: 292 us -> none  [the longest x1 193 us: per_device(): image_grad = lax.psum(partial_image, 'feat')]
    pallas_call x0 -> x1, Pallas kernels: none -> 104 us  [per_device(): pl.pallas_call(kernel, out_shape=(jax.ShapeDtypeStruct((1, 1), F32), jax....]
    reduce_scatter x1 -> x0, waiting for transfers between devices: 86.1 us -> none  [per_device(): lax.psum_scatter(grad_out, 'dp', scatter_dimension=0, tiled=True)]
    unnamed x7 -> x0, waiting for transfers between devices: 66.9 us -> none
    dot_general x10 -> x0, matrix products: 46.6 us -> none  [the longest x1 12.2 us: per_device(): jnp.dot(images, frequencies, preferred_element_type=jnp.float32)]
    psum x1 -> x0, blocking collectives: 37.1 us -> none  [per_device(): lax.psum(jnp.sum(mean_gap * mean_gap), 'feat') / (2.0 * total_feats)]
    all_gather x1 -> x0, blocking collectives: 25.1 us -> none  [per_device(): released = lax.all_gather(noisy, 'dp', axis=2, tiled=True)]
    unnamed x33 -> x2, local copies, waits for them, and re-layouts: 21.4 us -> 3.54 us
  transfers between devices with their start and end apart: 5 -> 0, of which waited for: 5 -> 0; matrix products, arithmetic and copies ran while one was open for 4% -> 0% of each run, Pallas kernels for 0% -> 0%
where the time goes in v1:
time: 111 us
  Pallas kernels  104 us (94%)
  local copies, waits for them, and re-layouts  4.79 us (4%)
  between operations  2.39 us (2%)
    pallas_call x1, Pallas kernels, per_device(): pl.pallas_call(kernel, out_shape=(jax.ShapeDtypeStruct((1, 1), F32), jax....  104 us
    unnamed x2, local copies, waits for them, and re-layouts  3.54 us

profile of v1, /device:TPU:1, one launch (start us, length us, event | category | flops | bytes accessed | tf_op | source)
XLA Modules:
  0.0 110.8 jit_solution(7197015982982462036)
XLA Ops:
  0.6 1.2 %reshape.15.lab_ref = s32[1,384]{1,0:T(1,128)} reshape(s32[384]{0:T(512)} %param.9) | data formatting | bytes 3072 | tf_op jit(solution)/shard_map/reshape | solution.py:570
  1.9 103.6 %feature_match.1 = (f32[1,1]{1,0:T(1,128)}, f32[16,1024]{1,0:T(8,128)}, f32[64,3072]{1,0:T(8,128)}) custom-call(bf16[384,3072]{1,0:T(8,128)(2,1)} %images_h.1, bf16[3072,1024]{1,0:T(8,128)(2,1)} %freq_h.1, bf16[1024,3072]{1,0:T(8,128)(2,1)} %gen_out_h.1, s32[1,384]{1,0:T(1,128)} %reshape.15.lab_ref, s32[1,256]{1,0:T(1,128)} %bitcast.2, ...), custom_call_target="tpu_custom_call" | custom-call | flops 12000000000 | bytes 17000000 | tf_op jit(solution)/shard_map/feature_match/pallas_call | solution.py:557
  106.1 1.5 %copy.15 = f32[16,1024]{1,0:T(8,128)} copy(f32[16,1024]{1,0:T(8,128)} %get-tuple-element.13) | data formatting | bytes 131072
  107.6 2.1 %copy.16 = f32[64,3072]{1,0:T(8,128)} copy(f32[64,3072]{1,0:T(8,128)} %get-tuple-element.14) | data formatting | bytes 1572864

commit v2 on v0

v2 whole, which is shorter than its diff:
```python
import functools

import jax
import jax.numpy as jnp
from jax import lax
from jax.experimental import pallas as pl
from jax.experimental.pallas import tpu as pltpu
from jax.sharding import PartitionSpec as P

MESH = pl.DeviceIdType.MESH
F32 = jnp.float32
BF16 = jnp.bfloat16

SIN = (6.28318284102346, -41.34142273936724, 81.59620932441723, -76.58030929887768, 41.20616782312917, -12.272323133322006)
COS = (0.999999989172567, -19.73920453212146, 64.93911898457917, -85.45016555726593, 60.16783176141255, -25.968313346422505, 6.5296104065360066)

N, D, FL, HID, Z, NI = 256, 3072, 1024, 1024, 256, 384
ROWS = N + NI
SUBS = (80, 32, 48, 32)
STARTS = (0, 80, 112, 160)
FIRST = ('x', 'z', 'x', 'x')
REL = (2, 1, 3, 0)
NS = len(SUBS)
D_OWN = sum(SUBS)
Q = 4 * NS
ORDER = (
    ("A", 0, 0), ("A", 0, 1), ("I", 2, 0), ("I", 2, 1), ("I", 2, 2), ("I", 2, 3), ("I", 3, 0), ("I", 3, 1),
    ("A", 0, 2), ("K", 0), ("A", 0, 3), ("A", 1, 0), ("A", 1, 1), ("A", 1, 2), ("K", 1), ("B", 0, 0), ("A", 1, 3),
    ("I", 3, 2), ("I", 3, 3), ("B", 0, 1), ("K", 2), ("A", 2, 0), ("B", 1, 0), ("A", 2, 1), ("A", 2, 2), ("A", 2, 3),
    ("A", 3, 0), ("A", 3, 1), ("K", 3), ("B", 0, 2), ("B", 1, 1), ("B", 1, 2), ("B", 0, 3), ("A", 3, 2), ("A", 3, 3),
    ("G1",), ("B", 2, 0), ("B", 2, 1), ("B", 1, 3), ("B", 2, 2), ("B", 2, 3), ("B", 3, 0), ("B", 3, 1), ("D", 0),
    ("D", 1), ("B", 3, 2), ("B", 3, 3), ("O1", 0), ("O1", 1), ("G2",), ("D", 2), ("O1", 2), ("D", 3), ("O2", 0),
    ("G3",), ("O2", 1), ("O1", 3), ("O2", 2), ("O2", 3), ("O3", 0), ("G4",), ("O3", 1), ("O3", 2), ("O3", 3), ("G5",),
    ("O4", 0), ("O4", 1), ("O4", 2), ("O4", 3), ("G6",),
)
NT = (((1,), (1,)), ((), ()))


def poly(coeffs, u):
    r = coeffs[-1] * u + coeffs[-2]
    for c in coeffs[-3::-1]:
        r = r * u + c
    return r


def cos_sin(phase):
    t = phase * 0.15915494309189535
    f = t - jnp.round(t)
    u = f * f
    return poly(COS, u), f * poly(SIN, u)


def split(v):
    hi = v.astype(BF16)
    return hi, (v - hi.astype(F32)).astype(BF16)


def mm(a, b):
    return jnp.dot(a, b, preferred_element_type=F32)


def mmt(a, b):
    return lax.dot_general(a, b, NT, preferred_element_type=F32)


def kernel(images_h, freq_h, gen_out_h, noise_h, lat_h, gin_h, lab_ref, glab_ref,
           loss_ref, gi_ref, go_ref,
           freq, gout, lhs, noise3, lat, gin_w, noise, hidden, q_s, qt, s_s, st, latt, oneh, onet, cosg, sing, gp, rsb, gapb, pg, ph,
           part, ohi, olo, gin, xa, xb, zr, gic, gid, gix, giz, gig, lvx, lvz, gt_p, goc, god, gfull,
           lsem, send, ar_r, xa_r, xb_r, zr_r, g_r, o_r):
    dp = lax.axis_index("dp")
    ft = lax.axis_index("feat")
    core = lax.rem(dp, 2)
    chip = dp // 2
    x = ft // 4
    zh = lax.rem(ft, 4)

    def xdev(k):
        return (dp, lax.rem(x + k, 4) * 4 + zh)

    def zdev(k):
        return (dp, x * 4 + lax.rem(zh + k, 4))

    def cdev(k):
        return (lax.rem(chip + k, 8) * 2 + core, ft)

    other = (chip * 2 + 1 - core, ft)

    def put(group, src, dst, rs, dev):
        pltpu.make_async_remote_copy(
            src_ref=src, dst_ref=dst, send_sem=send.at[group], recv_sem=rs, device_id=dev, device_id_type=MESH
        ).start()

    def arrived(ref, rs):
        pltpu.make_async_copy(ref, ref, rs).wait()

    loads = [pltpu.make_async_copy(gen_out_h.at[:, pl.ds(n * 512, 512)], gout.at[:, pl.ds(n * 512, 512)], lsem.at[n]) for n in range(6)]
    loads.append(pltpu.make_async_copy(images_h, lhs.at[pl.ds(N, NI)], lsem.at[6]))
    for n in range(4):
        loads.append(pltpu.make_async_copy(freq_h.at[:, pl.ds(n * 256, 256)], freq.at[:, pl.ds(n * 256, 256)], lsem.at[7 + n]))
    loads.append(pltpu.make_async_copy(lat_h, lat, lsem.at[11]))
    loads.append(pltpu.make_async_copy(gin_h, gin_w, lsem.at[12]))
    loads.append(pltpu.make_async_copy(noise_h, noise3, lsem.at[13]))
    loads[11].start()
    loads[12].start()
    for n in range(6):
        loads[n].start()
    loads[13].start()

    bar = pltpu.get_barrier_semaphore()

    def greet_dp(k, carry):
        pl.semaphore_signal(bar, inc=1, device_id=(lax.rem(dp + k, 16), ft), device_id_type=MESH)
        return carry

    lax.fori_loop(1, 16, greet_dp, 0)
    for k in (1, 2, 3):
        pl.semaphore_signal(bar, inc=1, device_id=xdev(k), device_id_type=MESH)
        pl.semaphore_signal(bar, inc=1, device_id=zdev(k), device_id_type=MESH)

    cls = lax.broadcasted_iota(jnp.int32, (32, N), 0)
    on_g = (jnp.where(cls < 16, cls, cls - 16) == glab_ref[...][None, :]).astype(F32)
    cls_g = lax.broadcasted_iota(jnp.int32, (16, N), 0)
    oneh[0:16, 0:N] = (cls_g == glab_ref[...][None, :]).astype(F32).astype(BF16)
    oneh[16:32, 0:N] = jnp.zeros((16, N), BF16)
    cls_d = lax.broadcasted_iota(jnp.int32, (16, NI), 0)
    oneh[0:16, N:ROWS] = jnp.zeros((16, NI), BF16)
    oneh[16:32, N:ROWS] = (cls_d == lab_ref[...][None, :]).astype(F32).astype(BF16)
    onet[...] = jnp.concatenate([on_g, jnp.zeros((96, N), F32)], axis=0).T.astype(BF16)
    loads[11].wait()
    latt[...] = lat[...].astype(F32).T.astype(BF16)
    loads[12].wait()

    pre = mm(lat[...], gin_w[...])
    sig = jax.nn.sigmoid(pre)
    hidden[...] = (pre * sig).astype(BF16)
    s_s[...] = sig * (1.0 + pre * (1.0 - sig))

    for n in range(6):
        loads[n].wait()
        if n < 5:
            loads[6 + n].start()
        cols = slice(n * 512, n * 512 + 512)
        out = jnp.tanh(mm(hidden[...], gout[:, cols]))
        lhs[0:N, cols] = out.astype(BF16)
        q_s[:, cols] = 1.0 - out * out
    loads[6].wait()

    def phase(n):
        loads[7 + n].wait()
        ph[n % 2] = mm(lhs[...], freq[:, n * 256 : n * 256 + 256])

    def sums(n):
        cols = slice(n * 256, n * 256 + 256)
        cs, sn = cos_sin(ph[n % 2])
        cosg[:, cols] = cs[0:N]
        sing[:, cols] = sn[0:N]
        for k, v in ((0, cs), (1, sn)):
            hi, lo = split(v)
            total = mm(oneh[...], hi) + mm(oneh[...], lo)
            gp[16 * k : 16 * k + 16, cols] = total[0:16] * (10.0 / 4096.0) - total[16:32] * (10.0 / 6144.0)

    def block(o):
        return pl.multiple_of(8 * (o // 4), 8), pl.multiple_of(128 * lax.rem(o, 4), 128)

    row_me, lane_me = block(dp)

    def ar_send(h):
        rsb[h, dp] = gp[pl.ds(row_me, 8), pl.ds(pl.multiple_of(h * 512 + lane_me, 128), 128)]

        def go(k, carry):
            peer = lax.rem(dp + k, 16)
            r, l = block(peer)
            put(0, gp.at[pl.ds(r, 8), pl.ds(pl.multiple_of(h * 512 + l, 128), 128)], rsb.at[h, dp], ar_r.at[h, 0], (peer, ft))
            return carry

        lax.fori_loop(1, 16, go, 0)

    def ar_spread(h):
        arrived(rsb.at[h, pl.ds(0, 15)], ar_r.at[h, 0])
        mine = gapb.at[h, pl.ds(row_me, 8), pl.ds(lane_me, 128)]
        mine[...] = jnp.sum(rsb[h], axis=0)

        def go(k, carry):
            put(0, mine, mine, ar_r.at[h, 1], (lax.rem(dp + k, 16), ft))
            return carry

        lax.fori_loop(1, 16, go, 0)

    def gap(h):
        arrived(rsb.at[h, pl.ds(0, 15)], ar_r.at[h, 1])
        cols = slice(h * 512, h * 512 + 512)
        g = gapb[h] - noise[:, cols]
        sq = g * g
        lv = sq[0:8] + sq[8:16] + sq[16:24] + sq[24:32]
        lv = lv[:, 0:128] + lv[:, 128:256] + lv[:, 256:384] + lv[:, 384:512]
        hi, lo = split(g * (160.0 / 4096.0))
        g0 = mm(onet[:, 0:32], jnp.concatenate([hi[0:16], lo[0:16]], axis=0))
        g1 = mm(onet[:, 0:32], jnp.concatenate([hi[16:32], lo[16:32]], axis=0))
        pg[:, cols] = (cosg[:, cols] * g1 - sing[:, cols] * g0).astype(BF16)
        return lv

    phase(0)
    phase(1)
    sums(0)
    phase(2)
    sums(1)
    pl.semaphore_wait(bar, 21)
    ar_send(0)
    phase(3)
    sums(2)
    ar_spread(0)
    sums(3)
    ar_send(1)

    def turn_q(n, carry):
        o = pl.multiple_of(n * 256, 256)
        qt[pl.ds(o, 256), :] = q_s[:, pl.ds(o, 256)].T
        return carry

    lax.fori_loop(0, 12, turn_q, 0)
    loads[13].wait()
    noise[...] = jnp.zeros_like(noise)
    for k in range(2):
        noise[16 * k : 16 * k + 10, :] = noise3[:, k, :]
    lv = gap(0)

    def first_half(n, carry):
        rows = pl.ds(pl.multiple_of(n * 768, 256), 768)
        part[rows, :] = mmt(freq[rows, 0:512], pg[:, 0:512])
        return carry

    lax.fori_loop(0, 4, first_half, 0)
    ar_spread(1)

    def turn_s(n, carry):
        o = pl.multiple_of(n * 256, 256)
        st[pl.ds(o, 256), :] = s_s[:, pl.ds(o, 256)].T
        return carry

    lax.fori_loop(0, 4, turn_s, 0)
    lv = lv + gap(1)

    def rows_at(r1, r2, s, half, rows):
        xr, zr = (r1, r2) if FIRST[s] == "x" else (r2, r1)
        base = lax.rem(x + xr, 4) * 768 + lax.rem(zh + zr, 4) * 192 + STARTS[s] + half
        return part.at[pl.ds(pl.multiple_of(base, 8), rows), :]

    def dev1(s, k):
        return xdev(k) if FIRST[s] == "x" else zdev(k)

    def dev2(s, k):
        return zdev(k) if FIRST[s] == "x" else xdev(k)

    def second_half(xr):
        rows = pl.ds(pl.multiple_of(lax.rem(x + xr, 4) * 768, 256), 768)
        part[rows, :] += mmt(freq[rows, 512:1024], pg[:, 512:1024])

    def do_i(s, k):
        h, q = SUBS[s] // 2, s * 4 + k
        for b in range(2):
            put(1, rows_at(2, REL[k], s, b * h, h), xa.at[q, b, pl.ds(0, h)], xa_r.at[q], dev1(s, (1, 3)[b]))

    def do_a(s, k):
        w, q = SUBS[s], s * 4 + k
        h = w // 2
        arrived(xa.at[q, :, pl.ds(0, h)], xa_r.at[q])
        for b in range(2):
            r = rows_at((1, 3)[b], REL[k], s, b * h, h)
            r[...] = r[...] + xa[q, b, 0:h]
            put(1, rows_at((1, 3)[b], REL[k], s, 0, w), xb.at[q, b, pl.ds(0, w)], xb_r.at[q], dev1(s, (1, 3)[b]))

    def do_b(s, k):
        w, q = SUBS[s], s * 4 + k
        arrived(xb.at[q, :, pl.ds(0, w)], xb_r.at[q])
        r = rows_at(0, REL[k], s, 0, w)
        r[...] = r[...] + xb[q, 0, 0:w] + xb[q, 1, 0:w]
        if k < 3:
            put(1, r, zr.at[s, k, pl.ds(0, w)], zr_r.at[s], dev2(s, REL[k]))

    def do_d(s):
        w = SUBS[s]
        arrived(zr.at[s, :, pl.ds(0, w)], zr_r.at[s])
        own = rows_at(0, 0, s, 0, w)[...] + zr[s, 0, 0:w] + zr[s, 1, 0:w] + zr[s, 2, 0:w]
        base = pl.multiple_of(ft * 192 + STARTS[s], 8)
        og = (own * qt[pl.ds(base, w), :]).astype(BF16)
        gt_p[s, 0:w, :] = mm(og, hidden[...])
        h = w // 2
        put(2, gt_p.at[s, pl.ds(pl.multiple_of((1 - core) * h, 8), h)], goc.at[s, pl.ds(0, h)], o_r.at[s, 0], other)

    second_half(2)
    for s in range(NS):
        if FIRST[s] == "x" and s < 1:
            for k in range(4):
                do_i(s, k)

    lvx[x] = lv
    for k in (1, 3, 2):
        put(3, lvx.at[x], lvx.at[x], g_r.at[6], xdev(k))

    for xr in (1, 3, 0):
        second_half(xr)
    for s in range(NS):
        if FIRST[s] == "z":
            for k in range(4):
                do_i(s, k)

    def factor(n, carry):
        rows = pl.ds(pl.multiple_of(n * 256, 256), 256)
        hi, lo = split(part[rows, :] * qt[rows, :])
        ohi[rows, :] = hi
        olo[rows, :] = lo
        return carry

    lax.fori_loop(0, 12, factor, 0)

    def rows_of(s, c):
        h = SUBS[s] // 2
        return pl.ds(pl.multiple_of(STARTS[s] + c * h, 8), h)

    def go1(s):
        h = SUBS[s] // 2
        mine = pl.ds(pl.multiple_of(core * h, 8), h)
        arrived(goc.at[s, pl.ds(0, h)], o_r.at[s, 0])
        r = gt_p.at[s, mine]
        r[...] = r[...] + goc[s, 0:h]
        for k in range(1, 8):
            peer = lax.rem(chip + k, 8)
            put(2, gt_p.at[s, mine, pl.ds(pl.multiple_of(peer * 128, 128), 128)], god.at[s, chip, pl.ds(0, h)], o_r.at[s, 1], cdev(k))
        god[s, chip, 0:h] = gt_p[s, mine, pl.ds(pl.multiple_of(chip * 128, 128), 128)]

    def go2(s):
        h = SUBS[s] // 2
        arrived(god.at[s, pl.ds(0, 7), pl.ds(0, h)], o_r.at[s, 1])
        gfull[ft, rows_of(s, core), :] = jnp.sum(god[s, :, 0:h], axis=0)
        at = gfull.at[ft, rows_of(s, core), :]
        for k in (1, 3, 2):
            put(2, at, at, o_r.at[s, 2], zdev(k))

    def go3(s):
        h = SUBS[s] // 2
        arrived(god.at[s, pl.ds(0, 3), pl.ds(0, h)], o_r.at[s, 2])
        at = gfull.at[pl.ds(x * 4, 4), rows_of(s, core), :]
        for k in (1, 3, 2):
            put(2, at, at, o_r.at[s, 3], xdev(k))

    def go4(s):
        arrived(gfull.at[pl.ds(0, 12), rows_of(s, core), :], o_r.at[s, 3])
        at = gfull.at[:, rows_of(s, core), :]
        put(2, at, at, o_r.at[s, 4], other)

    def back(n):
        rows = slice(n * 256, n * 256 + 256)
        bh = mm(gout[rows, :], ohi[...]) + mm(gout[rows, :], olo[...])
        hi, lo = split(bh * st[rows, :])
        g = mmt(latt[...], hi) + mmt(latt[...], lo)
        gin[:, :, :, rows] = g.reshape(8, 2, 16, 256)
        if n == 3:
            put(3, gin.at[:, 1 - core], gic, g_r.at[0], other)

    def gi1():
        arrived(gic, g_r.at[0])
        gin[:, core] = gin[:, core] + gic[...]
        for k in range(1, 8):
            put(3, gin.at[lax.rem(chip + k, 8), core], gid.at[chip], g_r.at[1], cdev(k))
        gid[chip] = gin[chip, core]

    def gi2():
        arrived(gid.at[pl.ds(0, 7)], g_r.at[1])
        gsum = jnp.sum(gid[...], axis=0)
        gic[0] = gsum
        for k in (1, 3, 2):
            cols = pl.ds(pl.multiple_of(lax.rem(x + k, 4) * 256, 256), 256)
            put(3, gic.at[0, :, cols], gix.at[x], g_r.at[2], xdev(k))
        gix[x] = gic[0, :, pl.ds(pl.multiple_of(x * 256, 256), 256)]
        arrived(lvx.at[pl.ds(0, 3)], g_r.at[6])
        lvz[zh] = jnp.sum(lvx[...], axis=0)
        for k in (1, 3, 2):
            put(3, lvz.at[zh], lvz.at[zh], g_r.at[7], zdev(k))

    def zblock(p):
        return pl.ds(pl.multiple_of(8 * (p // 2), 8), 8), pl.ds(pl.multiple_of(128 * lax.rem(p, 2), 128), 128)

    def gi3():
        arrived(gix.at[pl.ds(0, 3)], g_r.at[2])
        gic[1, :, 0:256] = jnp.sum(gix[...], axis=0)
        for k in (1, 3, 2):
            r, l = zblock(lax.rem(zh + k, 4))
            put(3, gic.at[1, r, l], giz.at[zh], g_r.at[3], zdev(k))
        r, l = zblock(zh)
        giz[zh] = gic[1, r, l]

    def gi4():
        arrived(giz.at[pl.ds(0, 3)], g_r.at[3])
        r, l = zblock(zh)
        gig[x, r, l] = jnp.sum(giz[...], axis=0)
        for k in (1, 3, 2):
            put(3, gig.at[x, r, l], gig.at[x, r, l], g_r.at[4], zdev(k))

    def gi5():
        arrived(giz.at[pl.ds(0, 3)], g_r.at[4])
        for k in (1, 3, 2):
            put(3, gig.at[x], gig.at[x], g_r.at[5], xdev(k))

    def gi6():
        arrived(gix.at[pl.ds(0, 3)], g_r.at[5])
        for p in range(4):
            gi_ref[:, p * 256 : p * 256 + 256] = gig[p]
        arrived(lvz.at[pl.ds(0, 3)], g_r.at[7])
        loss_ref[...] = jnp.sum(jnp.sum(lvz[...], axis=0), axis=(0, 1), keepdims=True) * (1.0 / 32768.0)

    steps = {"I": do_i, "A": do_a, "B": do_b, "D": do_d, "O1": go1, "O2": go2, "O3": go3, "O4": go4,
             "K": back, "G1": gi1, "G2": gi2, "G3": gi3, "G4": gi4, "G5": gi5, "G6": gi6}
    for name, *where in ORDER:
        steps[name](*where)
    for s in range(NS):
        arrived(gfull.at[:, rows_of(s, 1 - core), :], o_r.at[s, 4])

    def turn(p, carry):
        v = gfull[pl.ds(p * 2, 2)].reshape(384, 128).T
        go_ref[:, pl.ds(pl.multiple_of(p * 384, 128), 384)] = jnp.where(core == 0, v[0:64], v[64:128])
        return carry

    lax.fori_loop(0, 8, turn, 0)
    for group, rows in enumerate((240, 15 * D_OWN, 23 * D_OWN // 2, 1104)):
        arrived(part.at[pl.ds(0, rows)], send.at[group])


def hand_on(a, b, c, ao, bo, co):
    ao[...] = a[...]
    bo[...] = b[...]
    co[...] = c[...]


def per_device(images, labels, frequencies, privacy_noise, latents, gen_labels, gen_in, gen_out):
    vm = pl.BlockSpec(memory_space=pltpu.VMEM)
    hb = pl.BlockSpec(memory_space=pltpu.HBM)
    V = pltpu.VMEM
    dma = pltpu.SemaphoreType.DMA
    w = max(SUBS)
    h = w // 2
    scratch = [
        V((D, FL), BF16), V((HID, D), BF16), V((ROWS, D), BF16), V((10, 2, FL), F32), V((N, Z), BF16), V((Z, HID), BF16), V((32, FL), F32), V((N, HID), BF16),
        V((N, D), F32), V((D, N), F32), V((N, HID), F32), V((HID, N), F32), V((Z, N), BF16),
        V((32, ROWS), BF16), V((N, 128), BF16), V((N, FL), F32), V((N, FL), F32), V((32, FL), F32),
        V((2, 16, 8, 128), F32), V((2, 32, 512), F32), V((N, FL), BF16), V((2, ROWS, 256), F32),
        V((D, N), F32), V((D, N), BF16), V((D, N), BF16), V((8, 2, 16, HID), F32),
        V((Q, 2, h, N), F32), V((Q, 2, w, N), F32), V((NS, 3, w, N), F32),
        V((8, 16, HID), F32), V((8, 16, HID), F32), V((4, 16, 256), F32), V((4, 8, 128), F32), V((4, 16, 256), F32),
        V((4, 8, 128), F32), V((4, 8, 128), F32),
        V((NS, w, HID), F32), V((NS, h, HID), F32), V((NS, 8, h, 128), F32), V((16, 192, 128), F32),
    ]
    sems = [dma((14,)), dma((4,)), dma((2, 2)), dma((Q,)), dma((Q,)), dma((NS,)), dma((8,)), dma((NS, 5))]
    loss, gi, go = pl.pallas_call(
        kernel,
        out_shape=(
            jax.ShapeDtypeStruct((1, 1), F32),
            jax.ShapeDtypeStruct((16, HID), F32),
            jax.ShapeDtypeStruct((64, D), F32),
        ),
        in_specs=[hb] * 6 + [vm] * 2,
        out_specs=(vm, vm, vm),
        scratch_shapes=scratch + sems,
        compiler_params=pltpu.CompilerParams(collective_id=0, has_side_effects=True, vmem_limit_bytes=58 << 20),
        cost_estimate=pl.CostEstimate(flops=12_000_000_000, bytes_accessed=17_000_000, transcendentals=2_000_000),
        name="feature_match",
    )(images, frequencies, gen_out, privacy_noise, latents, gen_in, labels, gen_labels)
    loss, gi, go = pl.pallas_call(
        hand_on,
        out_shape=(
            jax.ShapeDtypeStruct((1, 1), F32),
            jax.ShapeDtypeStruct((16, HID), F32),
            jax.ShapeDtypeStruct((64, D), F32),
        ),
        in_specs=[vm] * 3,
        out_specs=(vm,) * 3,
        name="hand_on",
    )(loss, gi, go)
    return loss.reshape(()), gi, go


def solution(mesh):
    return jax.shard_map(
        per_device,
        mesh=mesh,
        in_specs=(
            P("dp", None),
            P("dp"),
            P(None, "feat"),
            P(None, None, "feat"),
            P("dp", None),
            P("dp"),
            P(),
            P(),
        ),
        out_specs=(P(), P("dp", None), P("dp", None)),
        check_vma=False,
    )
```

time: 609 us -> 94.3 us (0.15)
  waiting for transfers between devices: 445 us -> 0 us
  Pallas kernels: 0 us -> 93.5 us
  blocking collectives: 62.3 us -> 0 us
  matrix products: 46.6 us -> 0 us
  local copies, waits for them, and re-layouts: 25.8 us -> 0 us
  between operations: 15.8 us -> 0.64 us
  other arithmetic: 9.52 us -> 0 us
    psum x2 -> x0, waiting for transfers between devices: 292 us -> none  [the longest x1 193 us: per_device(): image_grad = lax.psum(partial_image, 'feat')]
    pallas_call x0 -> x2, Pallas kernels: none -> 93.5 us  [the longest x1 90.9 us: per_device(): pl.pallas_call(kernel, out_shape=(jax.ShapeDtypeStruct((1, 1), F32), jax....]
    reduce_scatter x1 -> x0, waiting for transfers between devices: 86.1 us -> none  [per_device(): lax.psum_scatter(grad_out, 'dp', scatter_dimension=0, tiled=True)]
    unnamed x7 -> x0, waiting for transfers between devices: 66.9 us -> none
    dot_general x10 -> x0, matrix products: 46.6 us -> none  [the longest x1 12.2 us: per_device(): jnp.dot(images, frequencies, preferred_element_type=jnp.float32)]
    psum x1 -> x0, blocking collectives: 37.1 us -> none  [per_device(): lax.psum(jnp.sum(mean_gap * mean_gap), 'feat') / (2.0 * total_feats)]
    all_gather x1 -> x0, blocking collectives: 25.1 us -> none  [per_device(): released = lax.all_gather(noisy, 'dp', axis=2, tiled=True)]
    unnamed x33 -> x0, local copies, waits for them, and re-layouts: 21.4 us -> none
  transfers between devices with their start and end apart: 5 -> 0, of which waited for: 5 -> 0; matrix products, arithmetic and copies ran while one was open for 4% -> 0% of each run, Pallas kernels for 0% -> 0%
where the time goes in v2:
time: 94.3 us; the launch traced here: 94.2 us
  Pallas kernels  93.5 us (99%)
    pallas_call x1, Pallas kernels, per_device(): pl.pallas_call(kernel, out_shape=(jax.ShapeDtypeStruct((1, 1), F32), jax....  90.9 us
    pallas_call x1, Pallas kernels, per_device(): pl.pallas_call(hand_on, out_shape=(jax.ShapeDtypeStruct((1, 1), F32), jax...  2.67 us

profile of v2, /device:TPU:1, one launch (start us, length us, event | category | flops | bytes accessed | tf_op | source)
XLA Modules:
  0.0 94.2 jit_solution(458291929090404939)
XLA Ops:
  0.6 90.9 %feature_match.1 = (f32[1,1]{1,0:T(1,128)}, f32[16,1024]{1,0:T(8,128)}, f32[64,3072]{1,0:T(8,128)}) custom-call(bf16[384,3072]{1,0:T(8,128)(2,1)} %images_h.1, bf16[3072,1024]{1,0:T(8,128)(2,1)} %freq_h.1, bf16[1024,3072]{1,0:T(8,128)(2,1)} %gen_out_h.1, f32[10,2,1024]{2,1,0:T(2,128)} %noise_h.1, bf16[256,256]{1,0:T(8,128)(2,1)} %lat_h.1, ...), custom_call_target="tpu_custom_call" | custom-call | flops 12000000000 | bytes 17000000 | tf_op jit(solution)/shard_map/feature_match/pallas_call | solution.py:454
  91.5 2.7 %hand_on.1 = (f32[1,1]{1,0:T(1,128)}, f32[16,1024]{1,0:T(8,128)}, f32[64,3072]{1,0:T(8,128)}) custom-call(f32[1,1]{1,0:T(1,128)} %get-tuple-element.9.a, f32[16,1024]{1,0:T(8,128)} %get-tuple-element.10.b, f32[64,3072]{1,0:T(8,128)} %get-tuple-element.11.c), custom_call_target="tpu_custom_call" | custom-call | tf_op jit(solution)/shard_map/hand_on/pallas_call | solution.py:468

commit v3 on v2

--- a/solution.py
+++ b/solution.py
@@ -16,22 +16,22 @@
 
 N, D, FL, HID, Z, NI = 256, 3072, 1024, 1024, 256, 384
 ROWS = N + NI
-SUBS = (80, 32, 48, 32)
-STARTS = (0, 80, 112, 160)
+SUBS = (64, 32, 64, 32)
+STARTS = (0, 64, 96, 160)
 FIRST = ('x', 'z', 'x', 'x')
 REL = (2, 1, 3, 0)
 NS = len(SUBS)
 D_OWN = sum(SUBS)
 Q = 4 * NS
 ORDER = (
-    ("A", 0, 0), ("A", 0, 1), ("I", 2, 0), ("I", 2, 1), ("I", 2, 2), ("I", 2, 3), ("I", 3, 0), ("I", 3, 1),
-    ("A", 0, 2), ("K", 0), ("A", 0, 3), ("A", 1, 0), ("A", 1, 1), ("A", 1, 2), ("K", 1), ("B", 0, 0), ("A", 1, 3),
-    ("I", 3, 2), ("I", 3, 3), ("B", 0, 1), ("K", 2), ("A", 2, 0), ("B", 1, 0), ("A", 2, 1), ("A", 2, 2), ("A", 2, 3),
-    ("A", 3, 0), ("A", 3, 1), ("K", 3), ("B", 0, 2), ("B", 1, 1), ("B", 1, 2), ("B", 0, 3), ("A", 3, 2), ("A", 3, 3),
-    ("G1",), ("B", 2, 0), ("B", 2, 1), ("B", 1, 3), ("B", 2, 2), ("B", 2, 3), ("B", 3, 0), ("B", 3, 1), ("D", 0),
-    ("D", 1), ("B", 3, 2), ("B", 3, 3), ("O1", 0), ("O1", 1), ("G2",), ("D", 2), ("O1", 2), ("D", 3), ("O2", 0),
-    ("G3",), ("O2", 1), ("O1", 3), ("O2", 2), ("O2", 3), ("O3", 0), ("G4",), ("O3", 1), ("O3", 2), ("O3", 3), ("G5",),
-    ("O4", 0), ("O4", 1), ("O4", 2), ("O4", 3), ("G6",),
+    ("A", 0, 0), ("A", 0, 1), ("I", 2, 0), ("I", 2, 1), ("A", 0, 2), ("I", 2, 2), ("K", 0), ("A", 0, 3), ("A", 1, 0),
+    ("K", 1), ("A", 1, 1), ("A", 1, 2), ("I", 2, 3), ("I", 3, 0), ("B", 0, 0), ("A", 1, 3), ("I", 3, 1), ("I", 3, 2),
+    ("I", 3, 3), ("K", 2), ("B", 0, 1), ("A", 2, 0), ("K", 3), ("B", 1, 0), ("A", 2, 1), ("B", 0, 2), ("B", 1, 1),
+    ("A", 2, 2), ("G1",), ("B", 0, 3), ("B", 1, 2), ("A", 2, 3), ("A", 3, 0), ("A", 3, 1), ("A", 3, 2), ("A", 3, 3),
+    ("B", 2, 0), ("B", 1, 3), ("B", 2, 1), ("D", 0), ("B", 2, 2), ("D", 1), ("O1", 0), ("B", 2, 3), ("B", 3, 0),
+    ("O1", 1), ("B", 3, 1), ("G1b",), ("B", 3, 2), ("B", 3, 3), ("D", 2), ("O1b", 0), ("O1", 2), ("O1b", 1), ("G2",),
+    ("O2", 0), ("D", 3), ("O2", 1), ("O1", 3), ("O1b", 2), ("O3", 0), ("O2", 2), ("O3", 1), ("G3",), ("O2", 3),
+    ("O4", 0), ("O3", 2), ("O4", 1), ("G4",), ("O4", 3), ("O4", 2),
 )
 NT = (((1,), (1,)), ((), ()))
 
@@ -65,8 +65,8 @@
 
 def kernel(images_h, freq_h, gen_out_h, noise_h, lat_h, gin_h, lab_ref, glab_ref,
            loss_ref, gi_ref, go_ref,
-           freq, gout, lhs, noise3, lat, gin_w, noise, hidden, q_s, qt, s_s, st, latt, oneh, onet, cosg, sing, gp, rsb, gapb, pg, ph,
-           part, ohi, olo, gin, xa, xb, zr, gic, gid, gix, giz, gig, lvx, lvz, gt_p, goc, god, gfull,
+           freq, gout, lhs, noise3, lat, gin_w, noise, hidden, q_s, qt, s_s, st, latt, oneh, onet, cosg, sing, gp, from_core0, from_core1, chips0, chips1, gap0, gap1, pg, ph,
+           part, ohi, gin, xa, xb, zr, gic, gid, gio, gix, gig, lvx, gt_p, goc, god, goy, goz, gfull,
            lsem, send, ar_r, xa_r, xb_r, zr_r, g_r, o_r):
     dp = lax.axis_index("dp")
     ft = lax.axis_index("feat")
@@ -85,6 +85,13 @@
         return (lax.rem(chip + k, 8) * 2 + core, ft)
 
     other = (chip * 2 + 1 - core, ft)
+    zl = chip // 4
+    y = lax.rem(chip, 4)
+
+    def ydev(k):
+        return ((zl * 4 + lax.rem(y + k, 4)) * 2 + core, ft)
+
+    zldev = (((1 - zl) * 4 + y) * 2 + core, ft)
 
     def put(group, src, dst, rs, dev):
         pltpu.make_async_remote_copy(
@@ -109,14 +116,12 @@
 
     bar = pltpu.get_barrier_semaphore()
 
-    def greet_dp(k, carry):
+    def greet(k, carry):
         pl.semaphore_signal(bar, inc=1, device_id=(lax.rem(dp + k, 16), ft), device_id_type=MESH)
-        return carry
-
-    lax.fori_loop(1, 16, greet_dp, 0)
-    for k in (1, 2, 3):
-        pl.semaphore_signal(bar, inc=1, device_id=xdev(k), device_id_type=MESH)
-        pl.semaphore_signal(bar, inc=1, device_id=zdev(k), device_id_type=MESH)
+        pl.semaphore_signal(bar, inc=1, device_id=(dp, lax.rem(ft + k, 16)), device_id_type=MESH)
+        return carry
+
+    lax.fori_loop(1, 16, greet, 0)
 
     cls = lax.broadcasted_iota(jnp.int32, (32, N), 0)
     on_g = (jnp.where(cls < 16, cls, cls - 16) == glab_ref[...][None, :]).astype(F32)
@@ -160,40 +165,34 @@
             total = mm(oneh[...], hi) + mm(oneh[...], lo)
             gp[16 * k : 16 * k + 16, cols] = total[0:16] * (10.0 / 4096.0) - total[16:32] * (10.0 / 6144.0)
 
-    def block(o):
-        return pl.multiple_of(8 * (o // 4), 8), pl.multiple_of(128 * lax.rem(o, 4), 128)
-
-    row_me, lane_me = block(dp)
-
-    def ar_send(h):
-        rsb[h, dp] = gp[pl.ds(row_me, 8), pl.ds(pl.multiple_of(h * 512 + lane_me, 128), 128)]
-
-        def go(k, carry):
-            peer = lax.rem(dp + k, 16)
-            r, l = block(peer)
-            put(0, gp.at[pl.ds(r, 8), pl.ds(pl.multiple_of(h * 512 + l, 128), 128)], rsb.at[h, dp], ar_r.at[h, 0], (peer, ft))
-            return carry
-
-        lax.fori_loop(1, 16, go, 0)
-
-    def ar_spread(h):
-        arrived(rsb.at[h, pl.ds(0, 15)], ar_r.at[h, 0])
-        mine = gapb.at[h, pl.ds(row_me, 8), pl.ds(lane_me, 128)]
-        mine[...] = jnp.sum(rsb[h], axis=0)
-
-        def go(k, carry):
-            put(0, mine, mine, ar_r.at[h, 1], (lax.rem(dp + k, 16), ft))
-            return carry
-
-        lax.fori_loop(1, 16, go, 0)
+    parts = ((slice(0, 512), from_core0, chips0, gap0), (slice(512, 1024), from_core1, chips1, gap1))
+    own_rows = pl.ds(pl.multiple_of(16 * core, 16), 16)
+    other_rows = pl.ds(pl.multiple_of(16 * (1 - core), 16), 16)
+
+    def ar1(h):
+        cols, got, _, _ = parts[h]
+        put(0, gp.at[other_rows, cols], got, ar_r.at[h, 0], other)
+
+    def ar2(h):
+        cols, got, chips, _ = parts[h]
+        arrived(got, ar_r.at[h, 0])
+        chips[chip] = gp[own_rows, cols] + got[...]
+        for k in range(1, 8):
+            put(0, chips.at[chip], chips.at[chip], ar_r.at[h, 1], cdev(k))
+
+    def ar3(h):
+        _, _, chips, whole = parts[h]
+        arrived(chips.at[pl.ds(0, 7)], ar_r.at[h, 1])
+        whole[own_rows, :] = jnp.sum(chips[...], axis=0)
+        put(0, whole.at[own_rows], whole.at[own_rows], ar_r.at[h, 2], other)
 
     def gap(h):
-        arrived(rsb.at[h, pl.ds(0, 15)], ar_r.at[h, 1])
-        cols = slice(h * 512, h * 512 + 512)
-        g = gapb[h] - noise[:, cols]
+        cols, _, _, whole = parts[h]
+        arrived(whole.at[other_rows], ar_r.at[h, 2])
+        g = whole[...] - noise[:, cols]
         sq = g * g
         lv = sq[0:8] + sq[8:16] + sq[16:24] + sq[24:32]
-        lv = lv[:, 0:128] + lv[:, 128:256] + lv[:, 256:384] + lv[:, 384:512]
+        lv = sum(lv[:, i : i + 128] for i in range(0, lv.shape[1], 128))
         hi, lo = split(g * (160.0 / 4096.0))
         g0 = mm(onet[:, 0:32], jnp.concatenate([hi[0:16], lo[0:16]], axis=0))
         g1 = mm(onet[:, 0:32], jnp.concatenate([hi[16:32], lo[16:32]], axis=0))
@@ -205,13 +204,14 @@
     sums(0)
     phase(2)
     sums(1)
-    pl.semaphore_wait(bar, 21)
-    ar_send(0)
+    pl.semaphore_wait(bar, 30)
+    ar1(0)
     phase(3)
     sums(2)
-    ar_spread(0)
+    ar2(0)
     sums(3)
-    ar_send(1)
+    ar1(1)
+    ar2(1)
 
     def turn_q(n, carry):
         o = pl.multiple_of(n * 256, 256)
@@ -219,11 +219,21 @@
         return carry
 
     lax.fori_loop(0, 12, turn_q, 0)
+    ar3(0)
     loads[13].wait()
     noise[...] = jnp.zeros_like(noise)
     for k in range(2):
         noise[16 * k : 16 * k + 10, :] = noise3[:, k, :]
+
+    def turn_s(n, carry):
+        o = pl.multiple_of(n * 256, 256)
+        st[pl.ds(o, 256), :] = s_s[:, pl.ds(o, 256)].T
+        return carry
+
+    lax.fori_loop(0, 4, turn_s, 0)
     lv = gap(0)
+
+    ar3(1)
 
     def first_half(n, carry):
         rows = pl.ds(pl.multiple_of(n * 768, 256), 768)
@@ -231,14 +241,7 @@
         return carry
 
     lax.fori_loop(0, 4, first_half, 0)
-    ar_spread(1)
-
-    def turn_s(n, carry):
-        o = pl.multiple_of(n * 256, 256)
-        st[pl.ds(o, 256), :] = s_s[:, pl.ds(o, 256)].T
-        return carry
-
-    lax.fori_loop(0, 4, turn_s, 0)
+
     lv = lv + gap(1)
 
     def rows_at(r1, r2, s, half, rows):
@@ -294,10 +297,12 @@
             for k in range(4):
                 do_i(s, k)
 
-    lvx[x] = lv
-    for k in (1, 3, 2):
-        put(3, lvx.at[x], lvx.at[x], g_r.at[6], xdev(k))
-
+    lvx[ft] = lv
+    def tell(k, carry):
+        put(3, lvx.at[ft], lvx.at[ft], g_r.at[4], (dp, lax.rem(ft + k, 16)))
+        return carry
+
+    lax.fori_loop(1, 16, tell, 0)
     for xr in (1, 3, 0):
         second_half(xr)
     for s in range(NS):
@@ -307,9 +312,7 @@
 
     def factor(n, carry):
         rows = pl.ds(pl.multiple_of(n * 256, 256), 256)
-        hi, lo = split(part[rows, :] * qt[rows, :])
-        ohi[rows, :] = hi
-        olo[rows, :] = lo
+        ohi[rows, :] = (part[rows, :] * qt[rows, :]).astype(BF16)
         return carry
 
     lax.fori_loop(0, 12, factor, 0)
@@ -324,18 +327,44 @@
         arrived(goc.at[s, pl.ds(0, h)], o_r.at[s, 0])
         r = gt_p.at[s, mine]
         r[...] = r[...] + goc[s, 0:h]
-        for k in range(1, 8):
-            peer = lax.rem(chip + k, 8)
-            put(2, gt_p.at[s, mine, pl.ds(pl.multiple_of(peer * 128, 128), 128)], god.at[s, chip, pl.ds(0, h)], o_r.at[s, 1], cdev(k))
-        god[s, chip, 0:h] = gt_p[s, mine, pl.ds(pl.multiple_of(chip * 128, 128), 128)]
+        if s == NS - 1:
+            for k in range(1, 8):
+                peer = lax.rem(chip + k, 8)
+                put(2, gt_p.at[s, mine, pl.ds(pl.multiple_of(peer * 128, 128), 128)], god.at[s, chip, pl.ds(0, h)], o_r.at[s, 1], cdev(k))
+            god[s, chip, 0:h] = gt_p[s, mine, pl.ds(pl.multiple_of(chip * 128, 128), 128)]
+            return
+        for t in range(2):
+            for k in (1, 3, 2):
+                cols = pl.ds(pl.multiple_of((t * 4 + lax.rem(y + k, 4)) * 128, 128), 128)
+                put(2, gt_p.at[s, mine, cols], god.at[s, t * 4 + y, pl.ds(0, h)], o_r.at[s, 1], ydev(k))
+            god[s, t * 4 + y, 0:h] = gt_p[s, mine, pl.ds(pl.multiple_of((t * 4 + y) * 128, 128), 128)]
+
+    def go1b(s):
+        h = SUBS[s] // 2
+        arrived(god.at[s, pl.ds(0, 6), pl.ds(0, h)], o_r.at[s, 1])
+        for t in range(2):
+            goy[s, t, 0:h] = jnp.sum(god[s, 4 * t : 4 * t + 4, 0:h], axis=0)
+        put(2, goy.at[s, 1 - zl, pl.ds(0, h)], goz.at[s, pl.ds(0, h)], o_r.at[s, 5], zldev)
 
     def go2(s):
         h = SUBS[s] // 2
-        arrived(god.at[s, pl.ds(0, 7), pl.ds(0, h)], o_r.at[s, 1])
-        gfull[ft, rows_of(s, core), :] = jnp.sum(god[s, :, 0:h], axis=0)
+        if s == NS - 1:
+            arrived(god.at[s, pl.ds(0, 7), pl.ds(0, h)], o_r.at[s, 1])
+            gfull[ft, rows_of(s, core), :] = jnp.sum(god[s, :, 0:h], axis=0)
+        else:
+            arrived(goz.at[s, pl.ds(0, h)], o_r.at[s, 5])
+            gfull[ft, rows_of(s, core), :] = goy[s, zl, 0:h] + goz[s, 0:h]
         at = gfull.at[ft, rows_of(s, core), :]
-        for k in (1, 3, 2):
-            put(2, at, at, o_r.at[s, 2], zdev(k))
+        if s < NS - 1:
+            for k in (1, 3, 2):
+                put(2, at, at, o_r.at[s, 2], zdev(k))
+        else:
+
+            def go(k, carry):
+                put(2, at, at, o_r.at[s, 3], (dp, lax.rem(ft + k, 16)))
+                return carry
+
+            lax.fori_loop(1, 16, go, 0)
 
     def go3(s):
         h = SUBS[s] // 2
@@ -345,14 +374,14 @@
             put(2, at, at, o_r.at[s, 3], xdev(k))
 
     def go4(s):
-        arrived(gfull.at[pl.ds(0, 12), rows_of(s, core), :], o_r.at[s, 3])
+        arrived(gfull.at[pl.ds(0, 12 if s < NS - 1 else 15), rows_of(s, core), :], o_r.at[s, 3])
         at = gfull.at[:, rows_of(s, core), :]
         put(2, at, at, o_r.at[s, 4], other)
 
     def back(n):
         rows = slice(n * 256, n * 256 + 256)
-        bh = mm(gout[rows, :], ohi[...]) + mm(gout[rows, :], olo[...])
-        hi, lo = split(bh * st[rows, :])
+        hb = mm(gout[rows, :], ohi[...]) * st[rows, :]
+        hi, lo = split(hb)
         g = mmt(latt[...], hi) + mmt(latt[...], lo)
         gin[:, :, :, rows] = g.reshape(8, 2, 16, 256)
         if n == 3:
@@ -361,56 +390,53 @@
     def gi1():
         arrived(gic, g_r.at[0])
         gin[:, core] = gin[:, core] + gic[...]
-        for k in range(1, 8):
-            put(3, gin.at[lax.rem(chip + k, 8), core], gid.at[chip], g_r.at[1], cdev(k))
-        gid[chip] = gin[chip, core]
+        for t in range(2):
+            for k in (1, 3, 2):
+                put(3, gin.at[t * 4 + lax.rem(y + k, 4), core], gid.at[t * 4 + y], g_r.at[1], ydev(k))
+            gid[t * 4 + y] = gin[t * 4 + y, core]
+
+    def gi1b():
+        arrived(gid.at[pl.ds(0, 6)], g_r.at[1])
+        for t in range(2):
+            gic[t] = jnp.sum(gid[4 * t : 4 * t + 4], axis=0)
+        put(3, gic.at[1 - zl], gio, g_r.at[5], zldev)
+
+    def block(p):
+        return pl.ds(pl.multiple_of(8 * lax.rem(p, 2), 8), 8), pl.ds(pl.multiple_of(128 * (p // 2), 128), 128)
 
     def gi2():
-        arrived(gid.at[pl.ds(0, 7)], g_r.at[1])
-        gsum = jnp.sum(gid[...], axis=0)
-        gic[0] = gsum
-        for k in (1, 3, 2):
-            cols = pl.ds(pl.multiple_of(lax.rem(x + k, 4) * 256, 256), 256)
-            put(3, gic.at[0, :, cols], gix.at[x], g_r.at[2], xdev(k))
-        gix[x] = gic[0, :, pl.ds(pl.multiple_of(x * 256, 256), 256)]
-        arrived(lvx.at[pl.ds(0, 3)], g_r.at[6])
-        lvz[zh] = jnp.sum(lvx[...], axis=0)
-        for k in (1, 3, 2):
-            put(3, lvz.at[zh], lvz.at[zh], g_r.at[7], zdev(k))
-
-    def zblock(p):
-        return pl.ds(pl.multiple_of(8 * (p // 2), 8), 8), pl.ds(pl.multiple_of(128 * lax.rem(p, 2), 128), 128)
+        arrived(gio, g_r.at[5])
+        gic[2] = gic[zl] + gio[...]
+
+        def go(k, carry):
+            peer = lax.rem(ft + k, 16)
+            r, l = block(peer)
+            put(3, gic.at[2, r, l], gix.at[ft], g_r.at[2], (dp, peer))
+            return carry
+
+        lax.fori_loop(1, 16, go, 0)
+        r, l = block(ft)
+        gix[ft] = gic[2, r, l]
 
     def gi3():
-        arrived(gix.at[pl.ds(0, 3)], g_r.at[2])
-        gic[1, :, 0:256] = jnp.sum(gix[...], axis=0)
-        for k in (1, 3, 2):
-            r, l = zblock(lax.rem(zh + k, 4))
-            put(3, gic.at[1, r, l], giz.at[zh], g_r.at[3], zdev(k))
-        r, l = zblock(zh)
-        giz[zh] = gic[1, r, l]
+        arrived(gix.at[pl.ds(0, 15)], g_r.at[2])
+        r, l = block(ft)
+        gig[r, l] = jnp.sum(gix[...], axis=0)
+
+        def go(k, carry):
+            put(3, gig.at[r, l], gig.at[r, l], g_r.at[3], (dp, lax.rem(ft + k, 16)))
+            return carry
+
+        lax.fori_loop(1, 16, go, 0)
 
     def gi4():
-        arrived(giz.at[pl.ds(0, 3)], g_r.at[3])
-        r, l = zblock(zh)
-        gig[x, r, l] = jnp.sum(giz[...], axis=0)
-        for k in (1, 3, 2):
-            put(3, gig.at[x, r, l], gig.at[x, r, l], g_r.at[4], zdev(k))
-
-    def gi5():
-        arrived(giz.at[pl.ds(0, 3)], g_r.at[4])
-        for k in (1, 3, 2):
-            put(3, gig.at[x], gig.at[x], g_r.at[5], xdev(k))
-
-    def gi6():
-        arrived(gix.at[pl.ds(0, 3)], g_r.at[5])
-        for p in range(4):
-            gi_ref[:, p * 256 : p * 256 + 256] = gig[p]
-        arrived(lvz.at[pl.ds(0, 3)], g_r.at[7])
-        loss_ref[...] = jnp.sum(jnp.sum(lvz[...], axis=0), axis=(0, 1), keepdims=True) * (1.0 / 32768.0)
-
-    steps = {"I": do_i, "A": do_a, "B": do_b, "D": do_d, "O1": go1, "O2": go2, "O3": go3, "O4": go4,
-             "K": back, "G1": gi1, "G2": gi2, "G3": gi3, "G4": gi4, "G5": gi5, "G6": gi6}
+        arrived(gix.at[pl.ds(0, 15)], g_r.at[3])
+        gi_ref[...] = gig[...]
+        arrived(lvx.at[pl.ds(0, 15)], g_r.at[4])
+        loss_ref[...] = jnp.sum(jnp.sum(lvx[...], axis=0), axis=(0, 1), keepdims=True) * (1.0 / 32768.0)
+
+    steps = {"I": do_i, "A": do_a, "B": do_b, "D": do_d, "O1": go1, "O1b": go1b, "O2": go2, "O3": go3, "O4": go4,
+             "K": back, "G1": gi1, "G1b": gi1b, "G2": gi2, "G3": gi3, "G4": gi4}
     for name, *where in ORDER:
         steps[name](*where)
     for s in range(NS):
@@ -422,8 +448,8 @@
         return carry
 
     lax.fori_loop(0, 8, turn, 0)
-    for group, rows in enumerate((240, 15 * D_OWN, 23 * D_OWN // 2, 1104)):
-        arrived(part.at[pl.ds(0, rows)], send.at[group])
+    for group, (rows, width) in enumerate(((576, 256), (15 * D_OWN, 256), (23 * D_OWN // 2, 256), (2280, 128))):
+        arrived(part.at[pl.ds(0, rows), pl.ds(0, width)], send.at[group])
 
 
 def hand_on(a, b, c, ao, bo, co):
@@ -443,14 +469,13 @@
         V((D, FL), BF16), V((HID, D), BF16), V((ROWS, D), BF16), V((10, 2, FL), F32), V((N, Z), BF16), V((Z, HID), BF16), V((32, FL), F32), V((N, HID), BF16),
         V((N, D), F32), V((D, N), F32), V((N, HID), F32), V((HID, N), F32), V((Z, N), BF16),
         V((32, ROWS), BF16), V((N, 128), BF16), V((N, FL), F32), V((N, FL), F32), V((32, FL), F32),
-        V((2, 16, 8, 128), F32), V((2, 32, 512), F32), V((N, FL), BF16), V((2, ROWS, 256), F32),
-        V((D, N), F32), V((D, N), BF16), V((D, N), BF16), V((8, 2, 16, HID), F32),
+        V((16, 512), F32), V((16, 512), F32), V((8, 16, 512), F32), V((8, 16, 512), F32), V((32, 512), F32), V((32, 512), F32), V((N, FL), BF16), V((2, ROWS, 256), F32),
+        V((D, N), F32), V((D, N), BF16), V((8, 2, 16, HID), F32),
         V((Q, 2, h, N), F32), V((Q, 2, w, N), F32), V((NS, 3, w, N), F32),
-        V((8, 16, HID), F32), V((8, 16, HID), F32), V((4, 16, 256), F32), V((4, 8, 128), F32), V((4, 16, 256), F32),
-        V((4, 8, 128), F32), V((4, 8, 128), F32),
-        V((NS, w, HID), F32), V((NS, h, HID), F32), V((NS, 8, h, 128), F32), V((16, 192, 128), F32),
+        V((8, 16, HID), F32), V((8, 16, HID), F32), V((16, HID), F32), V((16, 8, 128), F32), V((16, HID), F32), V((16, 8, 128), F32),
+        V((NS, w, HID), F32), V((NS, h, HID), F32), V((NS, 8, h, 128), F32), V((NS, 2, h, 128), F32), V((NS, h, 128), F32), V((16, 192, 128), F32),
     ]
-    sems = [dma((14,)), dma((4,)), dma((2, 2)), dma((Q,)), dma((Q,)), dma((NS,)), dma((8,)), dma((NS, 5))]
+    sems = [dma((14,)), dma((4,)), dma((2, 3)), dma((Q,)), dma((Q,)), dma((NS,)), dma((6,)), dma((NS, 6))]
     loss, gi, go = pl.pallas_call(
         kernel,
         out_shape=(

time: 94.3 us -> 89.6 us (0.950)
  Pallas kernels: 93.5 us -> 88.8 us
    pallas_call x1, Pallas kernels: 90.9 us -> 86.2 us  [per_device(): pl.pallas_call(kernel, out_shape=(jax.ShapeDtypeStruct((1, 1), F32), jax....]
where the time goes in v3:
time: 89.6 us; the launch traced here: 89.5 us
  Pallas kernels  88.8 us (99%)
    pallas_call x1, Pallas kernels, per_device(): pl.pallas_call(kernel, out_shape=(jax.ShapeDtypeStruct((1, 1), F32), jax....  86.2 us
    pallas_call x1, Pallas kernels, per_device(): pl.pallas_call(hand_on, out_shape=(jax.ShapeDtypeStruct((1, 1), F32), jax...  2.67 us

profile of v3, /device:TPU:1, one launch (start us, length us, event | category | flops | bytes accessed | tf_op | source)
XLA Modules:
  0.0 89.5 jit_solution(2681011621567791301)
XLA Ops:
  0.6 86.2 %feature_match.1 = (f32[1,1]{1,0:T(1,128)}, f32[16,1024]{1,0:T(8,128)}, f32[64,3072]{1,0:T(8,128)}) custom-call(bf16[384,3072]{1,0:T(8,128)(2,1)} %images_h.1, bf16[3072,1024]{1,0:T(8,128)(2,1)} %freq_h.1, bf16[1024,3072]{1,0:T(8,128)(2,1)} %gen_out_h.1, f32[10,2,1024]{2,1,0:T(2,128)} %noise_h.1, bf16[256,256]{1,0:T(8,128)(2,1)} %lat_h.1, ...), custom_call_target="tpu_custom_call" | custom-call | flops 12000000000 | bytes 17000000 | tf_op jit(solution)/shard_map/feature_match/pallas_call | solution.py:479
  86.8 2.7 %hand_on.1 = (f32[1,1]{1,0:T(1,128)}, f32[16,1024]{1,0:T(8,128)}, f32[64,3072]{1,0:T(8,128)}) custom-call(f32[1,1]{1,0:T(1,128)} %get-tuple-element.9.a, f32[16,1024]{1,0:T(8,128)} %get-tuple-element.10.b, f32[64,3072]{1,0:T(8,128)} %get-tuple-element.11.c), custom_call_target="tpu_custom_call" | custom-call | tf_op jit(solution)/shard_map/hand_on/pallas_call | solution.py:493

commit v4 on v3

--- a/solution.py
+++ b/solution.py
@@ -24,14 +24,77 @@
 D_OWN = sum(SUBS)
 Q = 4 * NS
 ORDER = (
-    ("A", 0, 0), ("A", 0, 1), ("I", 2, 0), ("I", 2, 1), ("A", 0, 2), ("I", 2, 2), ("K", 0), ("A", 0, 3), ("A", 1, 0),
-    ("K", 1), ("A", 1, 1), ("A", 1, 2), ("I", 2, 3), ("I", 3, 0), ("B", 0, 0), ("A", 1, 3), ("I", 3, 1), ("I", 3, 2),
-    ("I", 3, 3), ("K", 2), ("B", 0, 1), ("A", 2, 0), ("K", 3), ("B", 1, 0), ("A", 2, 1), ("B", 0, 2), ("B", 1, 1),
-    ("A", 2, 2), ("G1",), ("B", 0, 3), ("B", 1, 2), ("A", 2, 3), ("A", 3, 0), ("A", 3, 1), ("A", 3, 2), ("A", 3, 3),
-    ("B", 2, 0), ("B", 1, 3), ("B", 2, 1), ("D", 0), ("B", 2, 2), ("D", 1), ("O1", 0), ("B", 2, 3), ("B", 3, 0),
-    ("O1", 1), ("B", 3, 1), ("G1b",), ("B", 3, 2), ("B", 3, 3), ("D", 2), ("O1b", 0), ("O1", 2), ("O1b", 1), ("G2",),
-    ("O2", 0), ("D", 3), ("O2", 1), ("O1", 3), ("O1b", 2), ("O3", 0), ("O2", 2), ("O3", 1), ("G3",), ("O2", 3),
-    ("O4", 0), ("O3", 2), ("O4", 1), ("G4",), ("O4", 3), ("O4", 2),
+    ("A", 0, 0),
+    ("A", 0, 1),
+    ("I", 2, 0),
+    ("I", 2, 1),
+    ("A", 0, 2),
+    ("I", 2, 2),
+    ("K", 0),
+    ("A", 0, 3),
+    ("A", 1, 0),
+    ("K", 1),
+    ("A", 1, 1),
+    ("A", 1, 2),
+    ("I", 2, 3),
+    ("I", 3, 0),
+    ("B", 0, 0),
+    ("A", 1, 3),
+    ("I", 3, 1),
+    ("I", 3, 2),
+    ("I", 3, 3),
+    ("K", 2),
+    ("B", 0, 1),
+    ("A", 2, 0),
+    ("K", 3),
+    ("B", 1, 0),
+    ("A", 2, 1),
+    ("B", 0, 2),
+    ("B", 1, 1),
+    ("A", 2, 2),
+    ("G1",),
+    ("B", 0, 3),
+    ("B", 1, 2),
+    ("A", 2, 3),
+    ("A", 3, 0),
+    ("A", 3, 1),
+    ("A", 3, 2),
+    ("A", 3, 3),
+    ("B", 2, 0),
+    ("B", 1, 3),
+    ("B", 2, 1),
+    ("D", 0),
+    ("B", 2, 2),
+    ("D", 1),
+    ("O1", 0),
+    ("B", 2, 3),
+    ("B", 3, 0),
+    ("O1", 1),
+    ("B", 3, 1),
+    ("G1b",),
+    ("B", 3, 2),
+    ("B", 3, 3),
+    ("D", 2),
+    ("O1b", 0),
+    ("O1", 2),
+    ("O1b", 1),
+    ("G2",),
+    ("O2", 0),
+    ("D", 3),
+    ("O2", 1),
+    ("O1", 3),
+    ("O1b", 2),
+    ("O3", 0),
+    ("O2", 2),
+    ("O3", 1),
+    ("O2", 3),
+    ("G3",),
+    ("O4", 0),
+    ("O3", 2),
+    ("O4", 1),
+    ("O4", 3),
+    ("O4", 2),
+    ("G4",),
 )
 NT = (((1,), (1,)), ((), ()))
 

time: 89.6 us -> 89.7 us (level)
  no operation moved by 1% of the time
where the time goes in v4:
time: 89.7 us; the launch traced here: 89.6 us
  Pallas kernels  88.9 us (99%)
    pallas_call x1, Pallas kernels, per_device(): pl.pallas_call(kernel, out_shape=(jax.ShapeDtypeStruct((1, 1), F32), jax....  86.2 us
    pallas_call x1, Pallas kernels, per_device(): pl.pallas_call(hand_on, out_shape=(jax.ShapeDtypeStruct((1, 1), F32), jax...  2.67 us

profile of v4, /device:TPU:1, one launch (start us, length us, event | category | flops | bytes accessed | tf_op | source)
XLA Modules:
  0.0 89.6 jit_solution(5855143643574454158)
XLA Ops:
  0.6 86.2 %feature_match.1 = (f32[1,1]{1,0:T(1,128)}, f32[16,1024]{1,0:T(8,128)}, f32[64,3072]{1,0:T(8,128)}) custom-call(bf16[384,3072]{1,0:T(8,128)(2,1)} %images_h.1, bf16[3072,1024]{1,0:T(8,128)(2,1)} %freq_h.1, bf16[1024,3072]{1,0:T(8,128)(2,1)} %gen_out_h.1, f32[10,2,1024]{2,1,0:T(2,128)} %noise_h.1, bf16[256,256]{1,0:T(8,128)(2,1)} %lat_h.1, ...), custom_call_target="tpu_custom_call" | custom-call | flops 12000000000 | bytes 17000000 | tf_op jit(solution)/shard_map/feature_match/pallas_call | solution.py:542
  86.9 2.7 %hand_on.1 = (f32[1,1]{1,0:T(1,128)}, f32[16,1024]{1,0:T(8,128)}, f32[64,3072]{1,0:T(8,128)}) custom-call(f32[1,1]{1,0:T(1,128)} %get-tuple-element.9.a, f32[16,1024]{1,0:T(8,128)} %get-tuple-element.10.b, f32[64,3072]{1,0:T(8,128)} %get-tuple-element.11.c), custom_call_target="tpu_custom_call" | custom-call | tf_op jit(solution)/shard_map/hand_on/pallas_call | solution.py:556
